TPU v7x, 32 devices: a whole 2x2x4 slice. The times are simulated.
32 devices in a mesh: fsdp: 8 (over z, core), context: 2 (over y), tensor: 2 (over x).
Axes of the slice: x: 2, y: 2, z: 4, core: 2. Of those that a mesh axis runs over, the one named last changes fastest.
Arguments:
- block_input: bfloat16 [8192, 1024], P(('fsdp', 'context')), may hold values from -6 to 6
- cotangent: bfloat16 [8192, 1024], P(('fsdp', 'context')), may hold values from -6 to 6
- segments: int32 [8, 1024], P('fsdp'), may hold values from 0 to 2, as said below
- routes: int32 [8192, 8], P(('fsdp', 'context')), may hold values from 0 to 15, all different within a row; in each aligned block of 512 rows (0 to 511, 512 to 1023, ...) at most 320 rows name the same one
- attn_gain: bfloat16 [1024], P(('fsdp', 'context')), may hold values from 0.5 to 1.5
- query_weight: bfloat16 [1024, 1024], P(('fsdp', 'context'), 'tensor'), may hold values from -0.1875 to 0.1875
- key_weight: bfloat16 [1024, 512], P(('fsdp', 'context'), 'tensor'), may hold values from -0.1875 to 0.1875
- value_weight: bfloat16 [1024, 512], P(('fsdp', 'context'), 'tensor'), may hold values from -0.1875 to 0.1875
- out_weight: bfloat16 [1024, 1024], P('tensor', ('fsdp', 'context')), may hold values from -1.5 to 1.5
- ffn_gain: bfloat16 [1024], P(('fsdp', 'context')), may hold values from 0.5 to 1.5
- router_weight: bfloat16 [1024, 16], P(('fsdp', 'context')), may hold values from -0.09375 to 0.09375
- expert_gate: bfloat16 [16, 1024, 512], P('fsdp', None, 'tensor'), may hold values from -0.1875 to 0.1875
- expert_up: bfloat16 [16, 1024, 512], P('fsdp', None, 'tensor'), may hold values from -0.1875 to 0.1875
- expert_down: bfloat16 [16, 512, 1024], P('fsdp', 'tensor'), may hold values from -1 to 1
Outputs:
- output: bfloat16 [8192, 1024], P(('fsdp', 'context'))
- input_grad: float32 [8192, 1024], P(('fsdp', 'context'))
- grad_attn_gain: float32 [1024], P(('fsdp', 'context'))
- grad_query_weight: float32 [1024, 1024], P(('fsdp', 'context'), 'tensor')
- grad_key_weight: float32 [1024, 512], P(('fsdp', 'context'), 'tensor')
- grad_value_weight: float32 [1024, 512], P(('fsdp', 'context'), 'tensor')
- grad_out_weight: float32 [1024, 1024], P('tensor', ('fsdp', 'context'))
- grad_ffn_gain: float32 [1024], P(('fsdp', 'context'))
- grad_router_weight: float32 [1024, 16], P(('fsdp', 'context'))
- grad_expert_gate: float32 [16, 1024, 512], P('fsdp', 'context', 'tensor')
- grad_expert_up: float32 [16, 1024, 512], P('fsdp', 'context', 'tensor')
- grad_expert_down: float32 [16, 512, 1024], P('fsdp', 'tensor', 'context')
Inputs may be any that keep to these rules, and one draw needn't show every extreme that they name: `segments`: each sequence holds three documents in order (segment numbers 0, 1, 2, never falling); the first and the last are shorter than 512 tokens, so the middle one runs from the first device's positions to the last device's. `routes`: each token names 8 different experts; among the 512 rows of one device no expert is named more than 320 times, and in every draw some expert is named exactly 320 times there.
All inputs are finite; a program needn't handle non-finite values.
Results may differ from a plain program's by a relative error of at most 0.035.
Values may be sent and summed in bfloat16 or wider, within the bound.
A program may use at most 192 MiB of HBM per device.

v0:
```python
import jax
import jax.numpy as jnp
from jax import lax
from jax.sharding import PartitionSpec as P

HEAD_DIM = 64


precise = lax.Precision.HIGHEST
norm_eps = 1e-05
masked_score = -1e30


def seq_positions(segments):
    seg_length = segments.shape[-1]
    token_index = jnp.arange(seg_length, dtype=jnp.int32)
    is_start = jnp.concatenate(
        [jnp.ones(segments.shape[:-1] + (1,), dtype=bool), segments[..., 1:] != segments[..., :-1]],
        axis=-1,
    )
    seg_starts = lax.cummax(jnp.where(is_start, token_index, 0), axis=segments.ndim - 1)
    return token_index - seg_starts


def rotary_turn(values, positions, direction):
    half_dim = values.shape[-1] // 2
    inv_freq = 10000.0 ** (-2.0 * jnp.arange(half_dim, dtype=jnp.float32) / values.shape[-1])
    angles = direction * positions.astype(jnp.float32)[:, None] * inv_freq[None, :]
    cosine = jnp.cos(angles)[:, None, :]
    sine_part = jnp.sin(angles)[:, None, :]
    first_half = values[..., :half_dim]
    second_half = values[..., half_dim:]
    return jnp.concatenate(
        [
            first_half * cosine - second_half * sine_part,
            second_half * cosine + first_half * sine_part,
        ],
        axis=-1,
    )


def rms_scale(values):
    return lax.rsqrt(jnp.mean(values * values, axis=-1, keepdims=True) + norm_eps)


def per_device(
    block_input,
    cotangent,
    segments,
    routes,
    attn_gain,
    query_weight,
    key_weight,
    value_weight,
    out_weight,
    ffn_gain,
    router_weight,
    expert_gate,
    expert_up,
    expert_down,
):
    tok_rows = block_input.shape[0]
    width = block_input.shape[1]
    seq_len = segments.shape[1]
    offset = lax.axis_index("context") * tok_rows
    seq_segments = segments[0]
    all_positions = seq_positions(seq_segments)
    local_segments = lax.dynamic_slice_in_dim(seq_segments, offset, tok_rows)
    local_positions = lax.dynamic_slice_in_dim(all_positions, offset, tok_rows)
    local_index = offset + jnp.arange(tok_rows, dtype=jnp.int32)
    query_full, key_full, value_full, out_full, gain_one, gain_two, router_full = (
        lax.all_gather(query_weight, ("fsdp", "context"), axis=0, tiled=True),
        lax.all_gather(key_weight, ("fsdp", "context"), axis=0, tiled=True),
        lax.all_gather(value_weight, ("fsdp", "context"), axis=0, tiled=True),
        lax.all_gather(out_weight, ("fsdp", "context"), axis=1, tiled=True),
        lax.all_gather(attn_gain, ("fsdp", "context"), axis=0, tiled=True),
        lax.all_gather(ffn_gain, ("fsdp", "context"), axis=0, tiled=True),
        lax.all_gather(router_weight, ("fsdp", "context"), axis=0, tiled=True),
    )
    inputs = block_input.astype(jnp.float32)
    cot_float = cotangent.astype(jnp.float32)
    scale_one = rms_scale(inputs)
    normed = (inputs * scale_one * gain_one.astype(jnp.float32)).astype(jnp.bfloat16)
    q_heads = query_full.shape[1] // HEAD_DIM
    kv_heads = key_full.shape[1] // HEAD_DIM
    per_group = q_heads // kv_heads
    score_scale = HEAD_DIM ** (-0.5)
    q_lin = jnp.dot(normed, query_full, preferred_element_type=jnp.float32)
    k_lin = jnp.dot(normed, key_full, preferred_element_type=jnp.float32)
    v_lin = jnp.dot(normed, value_full, preferred_element_type=jnp.float32)
    queries = rotary_turn(q_lin.reshape(tok_rows, q_heads, HEAD_DIM), local_positions, 1.0).astype(
        jnp.bfloat16
    )
    keys_rot = rotary_turn(
        k_lin.reshape(tok_rows, kv_heads, HEAD_DIM), local_positions, 1.0
    ).astype(jnp.bfloat16)
    values = v_lin.astype(jnp.bfloat16)
    grouped = queries.reshape(tok_rows, kv_heads, per_group, HEAD_DIM)
    top_score = jnp.full((kv_heads, per_group, tok_rows), masked_score, jnp.float32)
    key_piece = lax.all_gather(keys_rot.reshape(tok_rows, -1), "context", axis=0, tiled=True)
    value_piece = lax.all_gather(values, "context", axis=0, tiled=True)
    piece_rows = key_piece.shape[0]
    key_piece = key_piece.reshape(piece_rows, kv_heads, HEAD_DIM)
    value_piece = value_piece.reshape(piece_rows, kv_heads, HEAD_DIM)
    key_index = jnp.arange(piece_rows, dtype=jnp.int32)
    allowed = (local_segments[:, None] == seq_segments[None, :]) & (
        local_index[:, None] >= key_index[None, :]
    )
    scores = (
        jnp.einsum("qkgd,nkd->kgqn", grouped, key_piece, preferred_element_type=jnp.float32)
        * score_scale
    )
    scores = jnp.where(allowed, scores, masked_score)
    new_top = jnp.maximum(top_score, jnp.max(scores, axis=-1))
    weights = jnp.where(allowed, jnp.exp(scores - new_top[..., None]), 0.0)
    weight_sum = jnp.sum(weights, axis=-1)
    context_sum = jnp.einsum(
        "kgqn,nkd->kgqd",
        weights.astype(jnp.bfloat16),
        value_piece,
        preferred_element_type=jnp.float32,
    )
    top_score, weight_sum, context_sum = (new_top, weight_sum, context_sum)
    context = context_sum / weight_sum[..., None]
    log_total = top_score + jnp.log(weight_sum)
    context_rows = jnp.transpose(context, (2, 0, 1, 3)).reshape(tok_rows, q_heads * HEAD_DIM)
    heads_out = context_rows.astype(jnp.bfloat16)
    attended = lax.psum(
        jnp.dot(heads_out, out_full, preferred_element_type=jnp.float32).astype(jnp.bfloat16),
        "tensor",
    ).astype(jnp.float32)
    residual = inputs + attended
    scale_two = rms_scale(residual)
    normed_two = (residual * scale_two * gain_two.astype(jnp.float32)).astype(jnp.bfloat16)
    logits = jnp.dot(normed_two, router_full, preferred_element_type=jnp.float32)
    selected = jnp.take_along_axis(logits, routes, axis=1)
    gate_probs = jax.nn.softmax(selected, axis=-1)
    experts_total = router_full.shape[1]
    top_count = routes.shape[1]
    local_experts = expert_gate.shape[0]
    fsdp_count = lax.axis_size("fsdp")
    capacity = tok_rows * top_count * 5 // (4 * experts_total)
    flat_expert = routes.reshape(-1)
    one_hot = (flat_expert[:, None] == jnp.arange(experts_total, dtype=jnp.int32)[None, :]).astype(
        jnp.int32
    )
    slot_rank = jnp.sum((jnp.cumsum(one_hot, axis=0) - 1) * one_hot, axis=1)
    slot_index = flat_expert * capacity + slot_rank
    route_token = jnp.arange(tok_rows * top_count, dtype=jnp.int32) // top_count
    slot_token = (
        jnp.full((experts_total * capacity,), tok_rows, jnp.int32).at[slot_index].set(route_token)
    )
    slot_gate = (
        jnp.zeros((experts_total * capacity,), jnp.float32)
        .at[slot_index]
        .set(gate_probs.reshape(-1))
    )
    padded_normed = jnp.concatenate([normed_two, jnp.zeros((1, width), jnp.bfloat16)], axis=0)
    padded_cot = jnp.concatenate([cot_float, jnp.zeros((1, width), jnp.float32)], axis=0)
    slot_cot = padded_cot[slot_token]
    send_rows = padded_normed[slot_token].reshape(fsdp_count, local_experts, capacity, width)
    send_grads = (
        (slot_gate[:, None] * slot_cot)
        .astype(jnp.bfloat16)
        .reshape(fsdp_count, local_experts, capacity, width)
    )
    got_rows, got_grads = (
        lax.all_to_all(send_rows, "fsdp", split_axis=0, concat_axis=0, tiled=True),
        lax.all_to_all(send_grads, "fsdp", split_axis=0, concat_axis=0, tiled=True),
    )
    gate_pre = jnp.einsum(
        "secd,edf->secf", got_rows, expert_gate, preferred_element_type=jnp.float32
    )
    up_pre = jnp.einsum("secd,edf->secf", got_rows, expert_up, preferred_element_type=jnp.float32)
    gate_act = jax.nn.silu(gate_pre)
    hidden = (gate_act * up_pre).astype(jnp.bfloat16)
    expert_out = jnp.einsum(
        "secf,efd->secd", hidden, expert_down, preferred_element_type=jnp.float32
    )
    hidden_grad = jnp.einsum(
        "secd,efd->secf", got_grads, expert_down, preferred_element_type=jnp.float32
    )
    sig_gate = jax.nn.sigmoid(gate_pre)
    gate_grad = (hidden_grad * up_pre * sig_gate * (1.0 + gate_pre * (1.0 - sig_gate))).astype(
        jnp.bfloat16
    )
    up_grad = (hidden_grad * gate_act).astype(jnp.bfloat16)
    row_grads = jnp.einsum(
        "secf,edf->secd", gate_grad, expert_gate, preferred_element_type=jnp.float32
    ) + jnp.einsum("secf,edf->secd", up_grad, expert_up, preferred_element_type=jnp.float32)
    down_term = jnp.einsum("secf,secd->efd", hidden, got_grads, preferred_element_type=jnp.float32)
    gate_term = jnp.einsum(
        "secd,secf->edf", got_rows, gate_grad, preferred_element_type=jnp.float32
    )
    up_term = jnp.einsum("secd,secf->edf", got_rows, up_grad, preferred_element_type=jnp.float32)
    grad_expert_gate, grad_expert_up, grad_expert_down = (
        lax.psum_scatter(
            gate_term.astype(jnp.bfloat16), "context", scatter_dimension=1, tiled=True
        ).astype(jnp.float32),
        lax.psum_scatter(
            up_term.astype(jnp.bfloat16), "context", scatter_dimension=1, tiled=True
        ).astype(jnp.float32),
        lax.psum_scatter(
            down_term.astype(jnp.bfloat16), "context", scatter_dimension=2, tiled=True
        ).astype(jnp.float32),
    )
    slot_total = experts_total * capacity
    back_out, back_grads = (
        lax.all_to_all(
            expert_out.astype(jnp.bfloat16), "fsdp", split_axis=0, concat_axis=0, tiled=True
        ).astype(expert_out.dtype),
        lax.all_to_all(
            row_grads.astype(jnp.bfloat16), "fsdp", split_axis=0, concat_axis=0, tiled=True
        ).astype(row_grads.dtype),
    )
    flat_out = back_out.reshape(slot_total, width)
    flat_grads = back_grads.reshape(slot_total, width)
    mixture = jax.ops.segment_sum(
        slot_gate[:, None] * flat_out, slot_token, num_segments=tok_rows + 1
    )[:tok_rows]
    slot_score = jnp.sum(slot_cot * flat_out, axis=1)
    gate_score = slot_score[slot_index].reshape(tok_rows, top_count)
    normed_two_grad = jax.ops.segment_sum(flat_grads, slot_token, num_segments=tok_rows + 1)[
        :tok_rows
    ]
    mixture, gate_score, normed_two_grad = (
        lax.psum(mixture.astype(jnp.bfloat16), "tensor").astype(jnp.float32),
        lax.psum(gate_score.astype(jnp.bfloat16), "tensor").astype(jnp.float32),
        lax.psum(normed_two_grad.astype(jnp.bfloat16), "tensor").astype(jnp.float32),
    )
    select_grad = gate_probs * (
        gate_score - jnp.sum(gate_probs * gate_score, axis=-1, keepdims=True)
    )
    logit_grad = jnp.sum(
        (routes[:, :, None] == jnp.arange(experts_total, dtype=jnp.int32)[None, None, :])
        * select_grad[:, :, None],
        axis=1,
    )
    router_term = jnp.dot(normed_two.astype(jnp.float32).T, logit_grad, precision=precise)
    normed_two_grad = normed_two_grad + jnp.dot(
        logit_grad, router_full.astype(jnp.float32).T, precision=precise
    )
    gain_term_two = jnp.sum(normed_two_grad * residual * scale_two, axis=0)
    weighted = normed_two_grad * gain_two.astype(jnp.float32)
    residual_grad = (
        cot_float
        + scale_two * weighted
        - residual * scale_two**3 * jnp.mean(weighted * residual, axis=-1, keepdims=True)
    )
    attended_grad = residual_grad.astype(jnp.bfloat16)
    out_term = jnp.dot(heads_out.T, attended_grad, preferred_element_type=jnp.float32)
    context_grad = jnp.dot(attended_grad, out_full.T, preferred_element_type=jnp.float32).astype(
        jnp.bfloat16
    )
    row_delta = jnp.sum(
        context_grad.astype(jnp.float32).reshape(tok_rows, q_heads, HEAD_DIM)
        * context_rows.reshape(tok_rows, q_heads, HEAD_DIM),
        axis=-1,
    )
    log_rows = jnp.transpose(log_total, (2, 0, 1)).reshape(tok_rows, q_heads)
    all_queries, all_context_grad, all_log, all_delta = (
        lax.all_gather(
            queries.reshape(tok_rows, -1).astype(jnp.float32).astype(jnp.bfloat16),
            "context",
            axis=0,
            tiled=True,
        ).astype(jnp.float32),
        lax.all_gather(
            context_grad.astype(jnp.float32).astype(jnp.bfloat16), "context", axis=0, tiled=True
        ).astype(jnp.float32),
        lax.all_gather(log_rows.astype(jnp.bfloat16), "context", axis=0, tiled=True).astype(
            log_rows.dtype
        ),
        lax.all_gather(row_delta.astype(jnp.bfloat16), "context", axis=0, tiled=True).astype(
            row_delta.dtype
        ),
    )
    all_queries = all_queries.astype(jnp.bfloat16)
    all_context_grad = all_context_grad.astype(jnp.bfloat16)
    q_block = 512
    q_blocks = seq_len // q_block
    value_heads = values.reshape(tok_rows, kv_heads, HEAD_DIM)

    def key_side(acc_pair, q_items):
        key_acc, value_acc = acc_pair
        q_part, grad_part, log_part, delta_part, seg_part, index_part = q_items
        q_part = q_part.reshape(q_block, kv_heads, per_group, HEAD_DIM)
        grad_part = grad_part.reshape(q_block, kv_heads, per_group, HEAD_DIM)
        allowed = (seg_part[:, None] == local_segments[None, :]) & (
            index_part[:, None] >= local_index[None, :]
        )
        scores = (
            jnp.einsum("qkgd,nkd->kgqn", q_part, keys_rot, preferred_element_type=jnp.float32)
            * score_scale
        )
        log_heads = jnp.transpose(log_part.reshape(q_block, kv_heads, per_group), (1, 2, 0))
        delta_heads = jnp.transpose(delta_part.reshape(q_block, kv_heads, per_group), (1, 2, 0))
        probs = jnp.where(allowed, jnp.exp(scores - log_heads[..., None]), 0.0)
        prob_grad = jnp.einsum(
            "qkgd,nkd->kgqn", grad_part, value_heads, preferred_element_type=jnp.float32
        )
        score_grad = (probs * (prob_grad - delta_heads[..., None])).astype(jnp.bfloat16)
        value_acc = value_acc + jnp.einsum(
            "kgqn,qkgd->nkd",
            probs.astype(jnp.bfloat16),
            grad_part,
            preferred_element_type=jnp.float32,
        )
        key_acc = (
            key_acc
            + jnp.einsum("kgqn,qkgd->nkd", score_grad, q_part, preferred_element_type=jnp.float32)
            * score_scale
        )
        query_part_grad = (
            jnp.einsum("kgqn,nkd->qkgd", score_grad, keys_rot, preferred_element_type=jnp.float32)
            * score_scale
        )
        return ((key_acc, value_acc), query_part_grad.reshape(q_block, q_heads * HEAD_DIM))

    q_items = (
        all_queries.reshape(q_blocks, q_block, -1),
        all_context_grad.reshape(q_blocks, q_block, -1),
        all_log.reshape(q_blocks, q_block, q_heads),
        all_delta.reshape(q_blocks, q_block, q_heads),
        seq_segments.reshape(q_blocks, q_block),
        jnp.arange(seq_len, dtype=jnp.int32).reshape(q_blocks, q_block),
    )
    acc_start = (
        jnp.zeros((tok_rows, kv_heads, HEAD_DIM), jnp.float32),
        jnp.zeros((tok_rows, kv_heads, HEAD_DIM), jnp.float32),
    )
    (key_rot_grad, value_sum_grad), query_terms = lax.scan(key_side, acc_start, q_items)
    query_rot_grad = lax.psum_scatter(
        query_terms.reshape(seq_len, q_heads * HEAD_DIM).astype(jnp.bfloat16),
        "context",
        scatter_dimension=0,
        tiled=True,
    ).astype(jnp.float32)
    query_grad = (
        rotary_turn(query_rot_grad.reshape(tok_rows, q_heads, HEAD_DIM), local_positions, -1.0)
        .reshape(tok_rows, -1)
        .astype(jnp.bfloat16)
    )
    key_grad = (
        rotary_turn(key_rot_grad, local_positions, -1.0).reshape(tok_rows, -1).astype(jnp.bfloat16)
    )
    value_grad = value_sum_grad.reshape(tok_rows, -1).astype(jnp.bfloat16)
    query_term = jnp.dot(normed.T, query_grad, preferred_element_type=jnp.float32)
    key_term = jnp.dot(normed.T, key_grad, preferred_element_type=jnp.float32)
    value_term = jnp.dot(normed.T, value_grad, preferred_element_type=jnp.float32)
    normed_grad = (
        jnp.dot(query_grad, query_full.T, preferred_element_type=jnp.float32)
        + jnp.dot(key_grad, key_full.T, preferred_element_type=jnp.float32)
        + jnp.dot(value_grad, value_full.T, preferred_element_type=jnp.float32)
    )
    normed_grad = lax.psum(normed_grad.astype(jnp.bfloat16), "tensor").astype(jnp.float32)
    gain_term_one = jnp.sum(normed_grad * inputs * scale_one, axis=0)
    weighted_one = normed_grad * gain_one.astype(jnp.float32)
    input_grad = (
        residual_grad
        + scale_one * weighted_one
        - inputs * scale_one**3 * jnp.mean(weighted_one * inputs, axis=-1, keepdims=True)
    )
    summed_grads = (
        lax.psum_scatter(query_term, ("fsdp", "context"), scatter_dimension=0, tiled=True),
        lax.psum_scatter(key_term, ("fsdp", "context"), scatter_dimension=0, tiled=True),
        lax.psum_scatter(value_term, ("fsdp", "context"), scatter_dimension=0, tiled=True),
        lax.psum_scatter(out_term, ("fsdp", "context"), scatter_dimension=1, tiled=True),
        lax.psum_scatter(gain_term_one, ("fsdp", "context"), scatter_dimension=0, tiled=True),
        lax.psum_scatter(gain_term_two, ("fsdp", "context"), scatter_dimension=0, tiled=True),
        lax.psum_scatter(router_term, ("fsdp", "context"), scatter_dimension=0, tiled=True),
    )
    output = (residual + mixture).astype(jnp.bfloat16)
    return (
        output,
        input_grad,
        summed_grads[4],
        summed_grads[0],
        summed_grads[1],
        summed_grads[2],
        summed_grads[3],
        summed_grads[5],
        summed_grads[6],
        grad_expert_gate,
        grad_expert_up,
        grad_expert_down,
    )


def solution(mesh):
    placed = (
        P(("fsdp", "context"), None),
        P(("fsdp", "context"), None),
        P("fsdp", None),
        P(("fsdp", "context"), None),
        P(("fsdp", "context")),
        P(("fsdp", "context"), "tensor"),
        P(("fsdp", "context"), "tensor"),
        P(("fsdp", "context"), "tensor"),
        P("tensor", ("fsdp", "context")),
        P(("fsdp", "context")),
        P(("fsdp", "context"), None),
        P("fsdp", None, "tensor"),
        P("fsdp", None, "tensor"),
        P("fsdp", "tensor", None),
    )
    return jax.shard_map(
        per_device,
        mesh=mesh,
        in_specs=placed,
        out_specs=(
            P(("fsdp", "context"), None),
            P(("fsdp", "context"), None),
            P(("fsdp", "context")),
            P(("fsdp", "context"), "tensor"),
            P(("fsdp", "context"), "tensor"),
            P(("fsdp", "context"), "tensor"),
            P("tensor", ("fsdp", "context")),
            P(("fsdp", "context")),
            P(("fsdp", "context"), None),
            P("fsdp", "context", "tensor"),
            P("fsdp", "context", "tensor"),
            P("fsdp", "tensor", "context"),
        ),
        check_vma=False,
    )
```

profile of v0, /device:TPU:0, one launch (start us, length us, event | category | flops | bytes accessed | tf_op | source)
XLA Modules:
  0.0 2022.1 jit_solution(13539998872086890941)
XLA Ops:
  17.5 35.1 %all-reduce.7 = (bf16[1024]{0:T(1024)(128)(2,1)S(1)}, bf16[1024]{0:T(1024)(128)(2,1)S(1)}) all-reduce(bf16[1024]{0:T(1024)(128)(2,1)S(1)} %dynamic-update-slice, bf16[1024]{0:T(1024)(128)(2,1)S(1)} %dynamic-update-slice.1), channel_id=1, replica_groups=mesh['fsdp'=8,'context'=2,'tensor'=2] {'fsdp','context'}, use_global_device_ids=true, to_apply=%add.2 | all-reduce | flops 2048 | bytes 8192
  54.3 4.6 reduce-window.19
  59.7 32.4 %all_gather.40 = bf16[1024,256]{1,0:T(8,128)(2,1)S(1)} all-gather(bf16[64,256]{1,0:T(8,128)(2,1)S(1)} %copy-done.60), channel_id=1, replica_groups=mesh['fsdp'=8,'context'=2,'tensor'=2] {'fsdp','context'}, dimensions={0}, use_global_device_ids=true | all-gather | bytes 557056 | tf_op jit(solution)/shard_map/all_gather | solution.py:73
  92.1 33.5 %all_gather.43 = bf16[1024,256]{1,0:T(8,128)(2,1)S(1)} all-gather(bf16[64,256]{1,0:T(8,128)(2,1)S(1)} %copy-done.61), channel_id=1, replica_groups=mesh['fsdp'=8,'context'=2,'tensor'=2] {'fsdp','context'}, dimensions={0}, use_global_device_ids=true | all-gather | bytes 557056 | tf_op jit(solution)/shard_map/all_gather | solution.py:74
  126.1 7.2 all_gather.44
  135.9 7.2 all_gather.41
  146.1 2.7 fusion.27
  149.0 4.0 fusion.28
  153.0 5.0 fusion.130
  158.1 3.1 convolution_convert_fusion
  161.3 15.5 scatter_custom_fusion
  176.8 24.2 %all-reduce.13.cloned.1.call-done = bf16[512,1024]{1,0:T(8,128)(2,1)} async-done(((bf16[512,1024]{1,0:T(8,128)(2,1)}), bf16[512,1024]{1,0:T(8,128)(2,1)}) %all-reduce.13.cloned.1.call-update) | async-done | bytes 1048592 | tf_op jit(solution)/shard_map/psum | solution.py:128
  204.8 22.5 %gather_fusion = bf16[5120,1024]{1,0:T(8,128)(2,1)} fusion(bf16[513,1024]{1,0:T(8,128)(2,1)S(1)} %concatenate.40, s32[5120]{0:T(1024)S(1)} %fusion.99), kind=kCustom, calls=%fused_computation | custom fusion | bytes 20992000 | tf_op jit(solution)/shard_map/gather | solution.py:161
  227.3 234.2 %all_to_all.20 = bf16[8,2,320,1024]{3,2,1,0:T(8,128)(2,1)S(1)} all-to-all(bf16[8,2,320,1024]{3,2,1,0:T(8,128)(2,1)} %bitcast.333), channel_id=1, replica_groups=mesh['fsdp'=8,'context'=2,'tensor'=2] {'fsdp'}, dimensions={0} | all-to-all | bytes 20971520 | tf_op jit(solution)/shard_map/all_to_all | solution.py:168
  461.5 4.0 copy-done.11
  465.5 2.9 fusion.37
  468.4 12.0 fusion.46
  481.9 5.4 convert_bitcast_fusion
  487.3 9.7 copy.165
  497.0 5.3 all-to-all-start.1
  502.3 197.3 %all-gather = bf16[16,64,16]{1,2,0:T(8,128)(2,1)S(1)} all-gather(bf16[1,64,16]{1,2,0:T(8,128)(2,1)S(1)} %bitcast.375), channel_id=1, replica_groups=mesh['fsdp'=8,'context'=2,'tensor'=2] {'fsdp','context'}, dimensions={0}, use_global_device_ids=true | all-gather | bytes 34816 | tf_op jit(solution)/shard_map/all_gather | solution.py:78
  701.6 22.8 %gather_fusion.1 = f32[5120,1024]{1,0:T(8,128)} fusion(f32[513,1024]{1,0:T(8,128)S(1)} %concatenate.41, s32[5120]{0:T(1024)S(1)} %fusion.99), kind=kCustom, calls=%fused_computation.1 | custom fusion | bytes 41963520 | tf_op jit(solution)/shard_map/gather | solution.py:160
  726.0 33.0 %gather_fusion.3 = f32[4096]{0:T(1024)S(1)} fusion(f32[512,16]{0,1:T(8,128)S(1)} %fusion.131, s32[4096]{0:T(1024)S(1)} %reshape.443), kind=kCustom, calls=%fused_computation.3 | custom fusion | bytes 65536 | tf_op jit(solution)/shard_map/jit(take_along_axis)/gather | solution.py:136
  759.4 10.9 multiply_reduce_fusion
  770.3 25.6 %gather_fusion.2 = bf16[4096]{0:T(1024)(128)(2,1)S(1)} fusion(bf16[5120]{0:T(1024)(128)(2,1)S(1)} %reduce_sum.128, s32[4096]{0:T(1024)S(1)} %broadcast_clamp_fusion), kind=kCustom, calls=%fused_computation.2 | custom fusion | bytes 32768 | tf_op jit(solution)/shard_map/gather | solution.py:222
  796.2 5.0 psum.38
  801.5 15.5 scatter_custom_fusion.1
  817.2 8.0 multiply_convert_fusion
  825.2 281.1 %all_to_all.21 = bf16[8,2,320,1024]{3,2,1,0:T(8,128)(2,1)S(1)} all-to-all(bf16[8,2,320,1024]{3,2,1,0:T(8,128)(2,1)S(1)} %multiply_convert_fusion), channel_id=1, replica_groups=mesh['fsdp'=8,'context'=2,'tensor'=2] {'fsdp'}, dimensions={0} | all-to-all | bytes 20971520 | tf_op jit(solution)/shard_map/all_to_all | solution.py:169
  1106.3 12.3 fusion.45
  1118.7 8.6 fusion.81
  1127.3 12.8 fusion.30
  1140.1 9.7 copy.167
  1149.8 235.5 %all_to_all.22 = bf16[8,2,320,1024]{3,2,1,0:T(8,128)(2,1)} all-to-all(bf16[8,2,320,1024]{3,2,1,0:T(8,128)(2,1)} %copy.167), channel_id=1, replica_groups=mesh['fsdp'=8,'context'=2,'tensor'=2] {'fsdp'}, dimensions={0} | all-to-all | bytes 20971520 | tf_op jit(solution)/shard_map/all_to_all | solution.py:212
  1385.2 44.7 %scatter_custom_fusion.3 = f32[513,1024]{1,0:T(8,128)} fusion(s32[5120]{0:T(1024)} %copy-done.51, bf16[5120,1024]{1,0:T(8,128)(2,1)} %bitcast.334, f32[]{:T(128)} %constant.63.clone.1), kind=kCustom, calls=%fused_computation.40 | custom fusion | flops 10485760 | bytes 12587520 | tf_op jit(solution)/shard_map/scatter-add | solution.py:223
  1430.0 2.9 slice.110
  1434.0 36.5 %all-reduce.15.cloned.1.call-done = bf16[512,1024]{1,0:T(8,128)(2,1)} async-done(((bf16[512,1024]{1,0:T(8,128)(2,1)}), bf16[512,1024]{1,0:T(8,128)(2,1)}) %all-reduce.15.cloned.1.call-update) | async-done | bytes 1048592 | tf_op jit(solution)/shard_map/psum | solution.py:229
  1470.5 3.0 multiply_reduce_fusion.1
  1478.6 4.4 all_gather.49
  1482.9 10.9 all-gather.10.cloned.1.call-done
  1496.1 4.6 all_gather.51
  1500.7 15.9 all-gather.12.cloned.1.call-done
  1518.8 29.7 %while.15 = (s32[]{:T(128)}, f32[512,4,64]{0,2,1:T(8,128)S(1)}, f32[512,4,64]{0,2,1:T(8,128)}, bf16[2,512,512]{2,1,0:T(8,128)(2,1)}, bf16[2,512,512]{2,1,0:T(8,1...) while((s32[]{:T(128)}, f32[512,4,64]{0,2,1:T(8,128)S(1)}, ...), condition=%wide.region_25.26_spmd.clone, body=%wide.region_24.25_spmd.clone.sunk | while | flops 1365115392 | bytes 51579124 | solution.py:332
  1523.6 2.9 fusion.198
  1526.5 3.4 fusion.196
  1538.0 3.9 fusion.198
  1541.9 3.4 fusion.196
  1548.7 3.2 fusion.134
  1552.0 9.0 bitcast_convert_fusion
  1561.3 9.9 bitcast_convert_fusion.1
  1571.3 9.9 bitcast_convert_fusion.2
  1581.3 11.7 bitcast_multiply_fusion
  1593.0 46.8 %scatter_custom_fusion.2 = f32[513,1024]{1,0:T(8,128)} fusion(s32[5120]{0:T(1024)} %copy-done.51, f32[5120,1024]{1,0:T(8,128)} %bitcast_multiply_fusion, f32[]{:T(128)} %constant.63.clone.1), kind=kCustom, calls=%fused_computation.119 | custom fusion | flops 5242880 | bytes 2101760 | tf_op jit(solution)/shard_map/scatter-add | solution.py:218
  1639.9 2.8 slice.111
  1654.0 3.7 fusion.93
  1664.2 9.3 reduce-scatter.24.cloned.1.call-done
  1675.7 21.1 %reduce-scatter.22.cloned.1.call-done = bf16[2,512,256]{2,1,0:T(8,128)(2,1)} async-done(((bf16[2,1024,256]{2,1,0:T(8,128)(2,1)}), bf16[2,512,256]{2,1,0:T(8,128)(2,1)}) %reduce-scatter.22.cloned.1.call-update) | async-done | bytes 524304 | tf_op jit(solution)/shard_map/reduce_scatter | solution.py:197
  1698.8 64.0 %all-reduce.17.cloned.1.call-done = (bf16[512,1024]{1,0:T(8,128)(2,1)}, bf16[512,1024]{1,0:T(8,128)(2,1)}) async-done(((bf16[512,1024]{1,0:T(8,128)(2,1)}, bf16[512,1024]{1,0:T(8,128)(2,1)}), (bf16[512,1024]{1,0:T(8,128)(2,1)}, bf16[512,1024]{1,0:T(8,128)(2,1)})) %all-reduce.17.cloned.1.call-update) | async-done | bytes 2097168 | tf_op jit(solution)/shard_map/psum | solution.py:227
  1764.9 33.8 %all-reduce.6 = (f32[1024]{0:T(1024)S(1)}, f32[1024]{0:T(1024)S(1)}) all-reduce(f32[1024]{0:T(1024)S(1)} %get-tuple-element.237, f32[1024]{0:T(1024)S(1)} %get-tuple-element.235), channel_id=3, replica_groups=mesh['fsdp'=8,'context'=2,'tensor'=2] {'fsdp','context'}, use_global_device_ids=true, to_apply=%region_30.31.clone | all-reduce | flops 2048 | bytes 16384
  1799.8 4.8 fusion.57
  1804.6 19.7 reduce-scatter.16.cloned.1.call-done
  1824.3 61.0 %reduce-scatter.18.cloned.1.call-done = f32[64,256]{1,0:T(8,128)} async-done(((f32[1024,256]{1,0:T(8,128)}), f32[64,256]{1,0:T(8,128)}) %reduce-scatter.18.cloned.1.call-update) | async-done | bytes 65552 | tf_op jit(solution)/shard_map/reduce_scatter | solution.py:367
  1885.3 64.8 %reduce-scatter.20.cloned.1.call-done = f32[512,64]{0,1:T(8,128)} async-done(((f32[512,1024]{0,1:T(8,128)}), f32[512,64]{0,1:T(8,128)}) %reduce-scatter.20.cloned.1.call-update) | async-done | bytes 131088 | tf_op jit(solution)/shard_map/reduce_scatter | solution.py:368
  1950.1 65.3 %reduce-scatter.14.cloned.1.call-done = f32[64,512]{1,0:T(8,128)} async-done(((f32[1024,512]{1,0:T(8,128)}), f32[64,512]{1,0:T(8,128)}) %reduce-scatter.14.cloned.1.call-update) | async-done | bytes 131088 | tf_op jit(solution)/shard_map/reduce_scatter | solution.py:365
  (314 shorter events, 79.7 us)
Async XLA Ops:
  7.2 474.7 %copy-start = (bf16[2,256,1024]{2,1,0:T(8,128)(2,1)S(1)}, bf16[2,256,1024]{2,1,0:T(8,128)(2,1)}, u32[]{:S(2)}) copy-start(bf16[2,256,1024]{2,1,0:T(8,128)(2,1)} %param.29) | copy-start | bytes 3145732
  7.2 52.5 %copy-start.60 = (bf16[64,256]{1,0:T(8,128)(2,1)S(1)}, bf16[64,256]{1,0:T(8,128)(2,1)}, u32[]{:S(2)}) copy-start(bf16[64,256]{1,0:T(8,128)(2,1)} %param.22) | copy-start | bytes 98308
  7.2 84.8 %copy-start.61 = (bf16[64,256]{1,0:T(8,128)(2,1)S(1)}, bf16[64,256]{1,0:T(8,128)(2,1)}, u32[]{:S(2)}) copy-start(bf16[64,256]{1,0:T(8,128)(2,1)} %param.23) | copy-start | bytes 98308
  7.2 136.6 %all-gather.6.cloned.1.call-start = ((), (), s32[]{:S(2)}) async-start(), calls=%async_computation.13 | async-start | bytes 1114112 | tf_op jit(solution)/shard_map/all_gather | solution.py:72
  7.9 150.1 %all-gather.8.cloned.1.call-start = ((), (), s32[]{:S(2)}) async-start(), calls=%async_computation.14 | async-start | bytes 1114112 | tf_op jit(solution)/shard_map/all_gather | solution.py:75
  8.7 192.3 %all-reduce.13.cloned.1.call-start = ((), (), s32[]{:S(2)}) async-start(), calls=%async_computation.15 | async-start | bytes 2097152 | tf_op jit(solution)/shard_map/psum | solution.py:128
  9.5 116.0 %copy-start.2 = (bf16[512,1024]{1,0:T(8,128)(2,1)S(1)}, bf16[512,1024]{1,0:T(8,128)(2,1)}, u32[]{:S(2)}) copy-start(bf16[512,1024]{1,0:T(8,128)(2,1)} %param.16) | copy-start | bytes 3145732
  12.3 131.0 %copy-start.47 = (s32[1,512]{1,0:T(1,128)}, s32[1,512]{1,0:T(1,128)S(1)}, u32[]{:S(2)}) copy-start(s32[1,512]{1,0:T(1,128)S(1)} %constant_dynamic-slice_fusion.6) | copy-start | bytes 6148
  52.6 91.3 %copy-start.54 = (f32[1024]{0:T(1024)}, f32[1024]{0:T(1024)S(1)}, u32[]{:S(2)}) copy-start(f32[1024]{0:T(1024)S(1)} %convert_element_type.192) | copy-start | bytes 12292
  53.2 90.7 %copy-start.62 = (f32[512]{0:T(512)}, f32[512]{0:T(512)S(1)}, u32[]{:S(2)}) copy-start(f32[512]{0:T(512)S(1)} %get-tuple-element.298) | copy-start | bytes 6148
  53.2 150.2 %copy-start.58 = (f32[1024]{0:T(1024)}, f32[1024]{0:T(1024)S(1)}, u32[]{:S(2)}) copy-start(f32[1024]{0:T(1024)S(1)} %convert_element_type.204) | copy-start | bytes 12292
  92.1 41.9 %copy-start.20 = (bf16[1024,256]{1,0:T(8,128)(2,1)}, bf16[1024,256]{1,0:T(8,128)(2,1)S(1)}, u32[]{:S(2)}) copy-start(bf16[1024,256]{1,0:T(8,128)(2,1)S(1)} %all_gather.40) | copy-start | bytes 1572868
  125.5 8.4 copy-start.18
  126.1 17.0 copy-start.41
  133.3 10.1 copy-start.49
  148.9 4.1 copy-start.52
  148.9 4.1 copy-start.40
  153.0 5.0 copy-start.56
  158.1 44.7 %copy-start.38 = (bf16[512,4,2,64]{0,3,2,1:T(8,128)(2,1)}, bf16[512,4,2,64]{0,3,2,1:T(8,128)(2,1)S(1)}, u32[]{:S(2)}) copy-start(bf16[512,4,2,64]{0,3,2,1:T(8,128)(2,1)S(1)} %get-tuple-element.307) | copy-start | bytes 1572868
  176.8 27.0 %copy-start.51 = (s32[5120]{0:T(1024)}, s32[5120]{0:T(1024)S(1)}, u32[]{:S(2)}) copy-start(s32[5120]{0:T(1024)S(1)} %scatter_custom_fusion) | copy-start | bytes 61444
  227.3 238.1 %copy-start.22 = (bf16[2,1024,256]{2,1,0:T(8,128)(2,1)S(1)}, bf16[2,1024,256]{2,1,0:T(8,128)(2,1)}, u32[]{:S(2)}) copy-start(bf16[2,1024,256]{2,1,0:T(8,128)(2,1)} %param.27) | copy-start | bytes 3145732
  461.5 4.0 copy-start.11
  468.4 12.0 copy-start.69
  497.0 5.4 copy-start.68
  497.0 202.8 %copy-start.35 = (s32[512,8]{0,1:T(8,128)S(1)}, s32[512,8]{0,1:T(8,128)}, u32[]{:S(2)}) copy-start(s32[512,8]{0,1:T(8,128)} %param.19) | copy-start | bytes 49156
  497.0 262.4 %all-to-all-start.1 = ((bf16[8,2,320,1024]{3,2,1,0:T(8,128)(2,1)}), bf16[8,2,320,1024]{3,2,1,0:T(8,128)(2,1)}, u32[]{:S(2)}, u32[]{:S(2)}) async-start(bf16[8,2,320,1024]{3,2,1,0:T(8,128)(2,1)} %copy.165), calls=%async_computation.1 | async-start | bytes 20971520 | tf_op jit(solution)/shard_map/all_to_all | solution.py:209
  502.3 968.2 %all-reduce.15.cloned.1.call-start = ((), (), s32[]{:S(2)}) async-start(), calls=%async_computation.16 | async-start | bytes 2097152 | tf_op jit(solution)/shard_map/psum | solution.py:229
  699.8 24.6 %copy-start.45 = (bf16[1024,16]{0,1:T(8,128)(2,1)}, bf16[1024,16]{0,1:T(8,128)(2,1)S(1)}, u32[]{:S(2)}) copy-start(bf16[1024,16]{0,1:T(8,128)(2,1)S(1)} %reshape.497) | copy-start | bytes 98308
  817.1 8.1 copy-start.43
  1106.3 12.4 copy-start.12
  1106.3 12.4 copy-start.23
  1118.7 8.6 copy-start.17
  1118.7 8.6 copy-start.25
  1430.0 3.0 copy-start.30
  1430.0 3.0 copy-start.32
  1430.0 40.5 %copy-start.3 = (bf16[512,1024]{1,0:T(8,128)(2,1)S(1)}, bf16[512,1024]{1,0:T(8,128)(2,1)}, u32[]{:S(2)}) copy-start(bf16[512,1024]{1,0:T(8,128)(2,1)} %param.16) | copy-start | bytes 3145732
  1430.0 40.5 %copy-start.8 = (bf16[512,1024]{1,0:T(8,128)(2,1)S(1)}, bf16[512,1024]{1,0:T(8,128)(2,1)}, u32[]{:S(2)}) copy-start(bf16[512,1024]{1,0:T(8,128)(2,1)} %all-reduce.13.cloned.1.call-done) | copy-start | bytes 3145732
  1430.0 40.5 %copy-start.46 = (bf16[1024,16]{0,1:T(8,128)(2,1)S(1)}, bf16[1024,16]{0,1:T(8,128)(2,1)}, u32[]{:S(2)}) copy-start(bf16[1024,16]{0,1:T(8,128)(2,1)} %copy-done.45) | copy-start | bytes 98308
  1430.0 40.5 %copy-start.59 = (f32[1024]{0:T(1024)S(1)}, f32[1024]{0:T(1024)}, u32[]{:S(2)}) copy-start(f32[1024]{0:T(1024)} %copy-done.58) | copy-start | bytes 12292
  1430.0 40.5 %copy-start.65 = (f32[512]{0:T(512)S(1)}, f32[512]{0:T(512)}, u32[]{:S(2)}) copy-start(f32[512]{0:T(512)} %copy-done.64) | copy-start | bytes 6148
  1432.9 60.9 %all-gather.10.cloned.1.call-start = ((), (), s32[]{:S(2)}) async-start(), calls=%async_computation.17 | async-start | bytes 1572864 | tf_op jit(solution)/shard_map/all_gather | solution.py:262
  1433.8 82.7 %all-gather.12.cloned.1.call-start = ((), (), s32[]{:S(2)}) async-start(), calls=%async_computation.18 | async-start | bytes 1572864 | tf_op jit(solution)/shard_map/all_gather | solution.py:268
  1434.0 39.5 %copy-start.15 = (bf16[512,1024]{1,0:T(8,128)(2,1)S(1)}, bf16[512,1024]{1,0:T(8,128)(2,1)}, u32[]{:S(2)}) copy-start(bf16[512,1024]{1,0:T(8,128)(2,1)} %param.17) | copy-start | bytes 3145732
  1434.0 39.5 %copy-start.67 = (f32[512]{0:T(512)S(1)}, f32[512]{0:T(512)}, u32[]{:S(2)}) copy-start(f32[512]{0:T(512)} %get-tuple-element.299) | copy-start | bytes 6148
  1477.2 41.7 %copy-start.5 = (bf16[512,4,64]{0,2,1:T(8,128)(2,1)S(1)}, bf16[512,4,64]{0,2,1:T(8,128)(2,1)}, u32[]{:S(2)}) copy-start(bf16[512,4,64]{0,2,1:T(8,128)(2,1)} %copy-done.4) | copy-start | bytes 786436
  1477.2 41.7 %copy-start.48 = (s32[1,512]{1,0:T(1,128)S(1)}, s32[1,512]{1,0:T(1,128)}, u32[]{:S(2)}) copy-start(s32[1,512]{1,0:T(1,128)} %copy-done.47) | copy-start | bytes 6148
  1477.2 168.5 %reduce-scatter.12.cloned.1.call-start = ((), (), s32[]{:S(2)}) async-start(), calls=%async_computation.19 | async-start | bytes 1572864 | tf_op jit(solution)/shard_map/reduce_scatter | solution.py:333
  1538.0 3.9 copy-start.42
  1548.6 112.1 %reduce-scatter.28.cloned.1.call-start = ((), (), s32[]{:S(2)}) async-start(), calls=%async_computation.27 | async-start | bytes 557056
  1551.9 110.2 %reduce-scatter.26.cloned.1.call-start = ((), (), s32[]{:S(2)}) async-start(), calls=%async_computation.26 | async-start | bytes 1572864 | tf_op jit(solution)/shard_map/reduce_scatter | solution.py:203
  1561.0 112.5 %reduce-scatter.24.cloned.1.call-start = ((), (), s32[]{:S(2)}) async-start(), calls=%async_computation.25 | async-start | bytes 1572864 | tf_op jit(solution)/shard_map/reduce_scatter | solution.py:200
  1571.3 10.0 copy-start.44
  1571.3 125.4 %reduce-scatter.22.cloned.1.call-start = ((), (), s32[]{:S(2)}) async-start(), calls=%async_computation.24 | async-start | bytes 1572864 | tf_op jit(solution)/shard_map/reduce_scatter | solution.py:197
  1581.2 181.5 %all-reduce.17.cloned.1.call-start = ((), (), s32[]{:S(2)}) async-start(), calls=%async_computation.28 | async-start | bytes 4194304 | tf_op jit(solution)/shard_map/psum | solution.py:227
  1593.0 50.7 %copy-start.36 = (f32[512,32]{0,1:T(8,128)S(1)}, f32[512,32]{0,1:T(8,128)}, u32[]{:S(2)}) copy-start(f32[512,32]{0,1:T(8,128)} %get-tuple-element.293) | copy-start | bytes 196612
  1593.0 50.7 %copy-start.37 = (f32[512,32]{0,1:T(8,128)S(1)}, f32[512,32]{0,1:T(8,128)}, u32[]{:S(2)}) copy-start(f32[512,32]{0,1:T(8,128)} %get-tuple-element.294) | copy-start | bytes 196612
  1639.9 4.0 copy-start.21
  1650.5 173.9 %reduce-scatter.16.cloned.1.call-start = ((), (), s32[]{:S(2)}) async-start(), calls=%async_computation.21 | async-start | bytes 1114112 | tf_op jit(solution)/shard_map/reduce_scatter | solution.py:366
  1652.2 233.1 %reduce-scatter.18.cloned.1.call-start = ((), (), s32[]{:S(2)}) async-start(), calls=%async_computation.22 | async-start | bytes 1114112 | tf_op jit(solution)/shard_map/reduce_scatter | solution.py:367
  1653.9 296.2 %reduce-scatter.20.cloned.1.call-start = ((), (), s32[]{:S(2)}) async-start(), calls=%async_computation.23 | async-start | bytes 2228224 | tf_op jit(solution)/shard_map/reduce_scatter | solution.py:368
  1657.7 357.7 %reduce-scatter.14.cloned.1.call-start = ((), (), s32[]{:S(2)}) async-start(), calls=%async_computation.20 | async-start | bytes 2228224 | tf_op jit(solution)/shard_map/reduce_scatter | solution.py:365
  1664.2 135.6 %copy-start.9 = (bf16[512,1024]{1,0:T(8,128)(2,1)S(1)}, bf16[512,1024]{1,0:T(8,128)(2,1)}, u32[]{:S(2)}) copy-start(bf16[512,1024]{1,0:T(8,128)(2,1)} %all-reduce.13.cloned.1.call-done) | copy-start | bytes 3145732
  1664.2 135.6 %copy-start.66 = (f32[512]{0:T(512)S(1)}, f32[512]{0:T(512)}, u32[]{:S(2)}) copy-start(f32[512]{0:T(512)} %get-tuple-element.297) | copy-start | bytes 6148
  1799.8 215.6 %copy-start.1 = (bf16[2,256,1024]{2,1,0:T(8,128)(2,1)S(1)}, bf16[2,256,1024]{2,1,0:T(8,128)(2,1)}, u32[]{:S(2)}) copy-start(bf16[2,256,1024]{2,1,0:T(8,128)(2,1)} %param.29) | copy-start | bytes 3145732
  (25 other events, 47.8 us)
Sparse Core Ops, SparseCore 0:
  10.3 40.8 all-gather.5
  53.4 37.7 all-gather.7
  161.4 39.6 all-reduce.12
  1433.0 37.3 all-reduce.14
  1472.4 21.3 all-gather.9
  1495.2 21.2 all-gather.11
  1548.7 20.2 reduce-scatter.11
  1573.0 55.7 reduce-scatter.27
  1631.1 19.3 reduce-scatter.25
  1653.2 20.3 reduce-scatter.23
  1676.4 20.2 reduce-scatter.21
  1699.6 63.0 all-reduce.16
  1766.9 57.3 reduce-scatter.15
  1828.8 56.4 reduce-scatter.17
  1889.4 60.6 reduce-scatter.19
  1954.7 60.6 reduce-scatter.13
where the time goes:
time: 2030 us; the launch traced here: 2020 us
  blocking collectives  1110 us (55%)
  waiting for transfers between devices  394 us (19%)
  local copies, waits for them, and re-layouts  194 us (10%)
  other arithmetic  159 us (8%)
  matrix products  140 us (7%)
    all_to_all x1, blocking collectives, per_device(): lax.all_to_all(send_grads, 'fsdp', split_axis=0, concat_axis=0, tiled=True)  281 us
    all_to_all x1, blocking collectives, per_device(): lax.all_to_all(row_grads.astype(jnp.bfloat16), 'fsdp', split_axis=0, conc...  235 us
    all_to_all x1, blocking collectives, per_device(): lax.all_to_all(send_rows, 'fsdp', split_axis=0, concat_axis=0, tiled=True)  234 us
    all_gather x1, blocking collectives, per_device(): lax.all_gather(router_weight, ('fsdp', 'context'), axis=0, tiled=True)  197 us
    unnamed x2, blocking collectives  68.8 us
    reduce_scatter x1, waiting for transfers between devices, per_device(): lax.psum_scatter(query_term, ('fsdp', 'context'), scatter_dimension=0, ti...  65.3 us
    reduce_scatter x1, waiting for transfers between devices, per_device(): lax.psum_scatter(out_term, ('fsdp', 'context'), scatter_dimension=1, tile...  64.8 us
    psum x1, waiting for transfers between devices, per_device(): lax.psum(mixture.astype(jnp.bfloat16), 'tensor').astype(jnp.float32)  64 us
  transfers between devices with their start and end apart: 17, of which 11 were waited for; matrix products, arithmetic and copies ran while one was open for 12% of the time, Pallas kernels for 0%

commit v1 on v0

v1 whole, which is shorter than its diff:
```python
import jax
import jax.numpy as jnp
from jax import lax
from jax.sharding import PartitionSpec as P

HEAD_DIM = 64

norm_eps = 1e-05
masked_score = -1e30
bf16 = jnp.bfloat16
f32 = jnp.float32
BOTH = ("fsdp", "context")


def rotary_tables(positions):
    half_dim = HEAD_DIM // 2
    inv_freq = 10000.0 ** (-2.0 * jnp.arange(half_dim, dtype=f32) / HEAD_DIM)
    angles = positions.astype(f32)[:, None] * inv_freq[None, :]
    return jnp.cos(angles)[:, None, :], jnp.sin(angles)[:, None, :]


def rotary_turn(values, cosine, sine_part):
    half_dim = HEAD_DIM // 2
    first_half = values[..., :half_dim]
    second_half = values[..., half_dim:]
    return jnp.concatenate(
        [
            first_half * cosine - second_half * sine_part,
            second_half * cosine + first_half * sine_part,
        ],
        axis=-1,
    )


def rms_scale(values):
    return lax.rsqrt(jnp.mean(values * values, axis=-1, keepdims=True) + norm_eps)


def dot(a, b):
    return jnp.dot(a, b, preferred_element_type=f32)


def dot_nt(a, b):
    return lax.dot_general(a, b, (((1,), (1,)), ((), ())), preferred_element_type=f32)


def dot_tn(a, b):
    return lax.dot_general(a, b, (((0,), (0,)), ((), ())), preferred_element_type=f32)


def swap_sum(part):
    count = lax.axis_size("tensor")
    low = part.astype(bf16)
    total = low.astype(f32)
    for step in range(1, count):
        total = total + lax.ppermute(
            low, "tensor", [(i, (i + step) % count) for i in range(count)]
        ).astype(f32)
    return total


def gather_rows(part, axis):
    count = lax.axis_size(axis)
    if count != 2:
        return lax.all_gather(part, axis, axis=0, tiled=True)
    other = lax.ppermute(part, axis, [(0, 1), (1, 0)])
    first = lax.axis_index(axis) == 0
    return jnp.concatenate(
        [jnp.where(first, part, other), jnp.where(first, other, part)], axis=0
    )


def scatter_sum(part, axis, dim):
    count = lax.axis_size(axis)
    if count != 2:
        return lax.psum_scatter(
            part.astype(bf16), axis, scatter_dimension=dim, tiled=True
        ).astype(f32)
    half = part.shape[dim] // 2
    me = lax.axis_index(axis)
    kept = lax.dynamic_slice_in_dim(part, me * half, half, axis=dim)
    sent = lax.dynamic_slice_in_dim(part, (1 - me) * half, half, axis=dim).astype(bf16)
    return kept + lax.ppermute(sent, axis, [(0, 1), (1, 0)]).astype(f32)


def per_device(
    block_input,
    cotangent,
    segments,
    routes,
    attn_gain,
    query_weight,
    key_weight,
    value_weight,
    out_weight,
    ffn_gain,
    router_weight,
    expert_gate,
    expert_up,
    expert_down,
):
    tok_rows, width = block_input.shape
    seq_len = segments.shape[1]
    fsdp_count = lax.axis_size("fsdp")
    local_experts, _, hid = expert_gate.shape
    experts_total = local_experts * fsdp_count
    q_cols, k_cols = query_weight.shape[1], key_weight.shape[1]
    o_cols = out_weight.shape[0]
    w_rows = query_weight.shape[0]
    qkv_cols = q_cols + 2 * k_cols
    q_heads, kv_heads = q_cols // HEAD_DIM, k_cols // HEAD_DIM
    per_group = q_heads // kv_heads
    score_scale = HEAD_DIM ** (-0.5)

    small = jnp.concatenate(
        [
            router_weight,
            attn_gain[:, None],
            ffn_gain[:, None],
            jnp.zeros((w_rows, 128 - (experts_total + 2) % 128), bf16),
        ],
        axis=1,
    )
    packed = jnp.concatenate([query_weight, key_weight, value_weight, out_weight.T, small], axis=1)
    full = lax.all_gather(packed, BOTH, axis=0, tiled=True)
    qkv_full = full[:, :qkv_cols]
    out_full_t = full[:, qkv_cols : qkv_cols + o_cols]
    tail = full[:, qkv_cols + o_cols :]
    router_full = tail[:, :experts_total]
    gain_one = tail[:, experts_total].astype(f32)
    gain_two = tail[:, experts_total + 1].astype(f32)

    seq_inputs = gather_rows(block_input, "context")

    named = jnp.any(
        routes[:, :, None] == jnp.arange(experts_total, dtype=jnp.int32)[None, None, :], axis=1
    )
    mask_rows = tok_rows * experts_total // width
    cot_pack = jnp.concatenate(
        [cotangent, named.astype(bf16).reshape(mask_rows, width)], axis=0
    )
    cot_got = lax.all_gather(cot_pack, "fsdp", axis=0, tiled=True).reshape(
        fsdp_count, tok_rows + mask_rows, width
    )

    offset = lax.axis_index("context") * tok_rows
    seq_segments = segments[0]
    seq_index = jnp.arange(seq_len, dtype=jnp.int32)
    starts = jnp.sum(
        (seq_segments[None, :] < seq_segments[:, None]).astype(jnp.int32), axis=1
    )
    cosine, sine_part = rotary_tables(seq_index - starts)
    local_segments = lax.dynamic_slice_in_dim(seq_segments, offset, tok_rows)
    local_index = offset + jnp.arange(tok_rows, dtype=jnp.int32)
    local_cos = lax.dynamic_slice_in_dim(cosine, offset, tok_rows)
    local_sin = lax.dynamic_slice_in_dim(sine_part, offset, tok_rows)

    inputs = block_input.astype(f32)
    cot_float = cotangent.astype(f32)
    scale_one = rms_scale(inputs)
    seq_float = seq_inputs.astype(f32)
    seq_normed = (seq_float * rms_scale(seq_float) * gain_one).astype(bf16)
    normed = lax.dynamic_slice_in_dim(seq_normed, offset, tok_rows)
    q_lin = dot(normed, qkv_full[:, :q_cols])
    kv_lin = dot(seq_normed, qkv_full[:, q_cols:])
    queries = rotary_turn(
        q_lin.reshape(tok_rows, q_heads, HEAD_DIM), local_cos, local_sin
    ).astype(bf16)
    keys = rotary_turn(
        kv_lin[:, :k_cols].reshape(seq_len, kv_heads, HEAD_DIM), cosine, sine_part
    ).astype(bf16)
    values = kv_lin[:, k_cols:].reshape(seq_len, kv_heads, HEAD_DIM).astype(bf16)
    grouped = queries.reshape(tok_rows, kv_heads, per_group, HEAD_DIM)
    allowed = (local_segments[:, None] == seq_segments[None, :]) & (
        local_index[:, None] >= seq_index[None, :]
    )
    scores = (
        jnp.einsum("qkgd,nkd->kgqn", grouped, keys, preferred_element_type=f32) * score_scale
    )
    scores = jnp.where(allowed, scores, masked_score)
    top = jnp.max(scores, axis=-1, keepdims=True)
    weights = jnp.where(allowed, jnp.exp(scores - top), 0.0)
    weight_sum = jnp.sum(weights, axis=-1, keepdims=True)
    probs = (weights / weight_sum).astype(bf16)
    context = jnp.einsum("kgqn,nkd->qkgd", probs, values, preferred_element_type=f32)
    context_rows = context.reshape(tok_rows, q_cols)
    heads_out = context_rows.astype(bf16)
    attended = swap_sum(dot_nt(heads_out, out_full_t))
    residual = inputs + attended
    scale_two = rms_scale(residual)
    normed_two = (residual * scale_two * gain_two).astype(bf16)

    all_normed = lax.all_gather(normed_two, "fsdp", axis=0, tiled=True)
    all_tokens = all_normed.shape[0]
    all_cot = cot_got[:, :tok_rows].reshape(all_tokens, width)
    all_named = cot_got[:, tok_rows:].reshape(all_tokens, experts_total) > 0

    def gates(rows, mask):
        logits = jnp.where(mask, dot(rows, router_full), masked_score)
        raised = jnp.where(
            mask, jnp.exp(logits - jnp.max(logits, axis=-1, keepdims=True)), 0.0
        )
        return raised / jnp.sum(raised, axis=-1, keepdims=True)

    gate_probs = gates(normed_two, named)
    all_gates = lax.dynamic_slice_in_dim(
        gates(all_normed, all_named), lax.axis_index("fsdp") * local_experts, local_experts, axis=1
    )
    gate_parts, up_parts, hid_parts, score_parts = [], [], [], []
    for e in range(local_experts):
        gate_pre = dot(all_normed, expert_gate[e])
        up_pre = dot(all_normed, expert_up[e])
        cot_hid = dot_nt(all_cot, expert_down[e])
        gate_e = all_gates[:, e : e + 1]
        sig_gate = jax.nn.sigmoid(gate_pre)
        gate_act = gate_pre * sig_gate
        hidden = gate_act * up_pre
        score_parts.append(jnp.sum(hidden * cot_hid, axis=1, keepdims=True))
        hid_parts.append((gate_e * hidden).astype(bf16))
        hidden_grad = gate_e * cot_hid
        gate_parts.append(
            (hidden_grad * up_pre * sig_gate * (1.0 + gate_pre * (1.0 - sig_gate))).astype(bf16)
        )
        up_parts.append((hidden_grad * gate_act).astype(bf16))
    own = lax.axis_index("fsdp") * local_experts + jnp.arange(local_experts, dtype=jnp.int32)
    spread = (own[:, None] == jnp.arange(experts_total, dtype=jnp.int32)[None, :]).astype(f32)
    score_wide = sum(score_parts[e] * spread[e][None, :] for e in range(local_experts))

    row_grads = sum(
        dot_nt(gate_parts[e], expert_gate[e]) + dot_nt(up_parts[e], expert_up[e])
        for e in range(local_experts)
    ).astype(bf16)
    back_pack = jnp.concatenate(
        [
            row_grads.reshape(fsdp_count, tok_rows, width),
            score_wide.astype(bf16).reshape(fsdp_count, mask_rows, width),
        ],
        axis=1,
    )
    back = lax.psum_scatter(
        back_pack.reshape(fsdp_count * (tok_rows + mask_rows), width),
        "fsdp",
        scatter_dimension=0,
        tiled=True,
    )
    mixture_part = sum(dot(hid_parts[e], expert_down[e]) for e in range(local_experts)).astype(
        bf16
    )
    mixture_part, back = lax.optimization_barrier((mixture_part, back))
    mixture = lax.psum_scatter(mixture_part, "fsdp", scatter_dimension=0, tiled=True)

    gate_term = jnp.stack([dot_tn(all_normed, gate_parts[e]) for e in range(local_experts)])
    up_term = jnp.stack([dot_tn(all_normed, up_parts[e]) for e in range(local_experts)])
    down_term = jnp.stack([dot_tn(hid_parts[e], all_cot) for e in range(local_experts)])
    grad_expert_gate = scatter_sum(gate_term, "context", 1)
    grad_expert_up = scatter_sum(up_term, "context", 1)
    grad_expert_down = scatter_sum(down_term, "context", 2)

    back_sum = swap_sum(back)
    gate_score = back_sum[tok_rows:].reshape(tok_rows, experts_total)
    logit_grad = gate_probs * (
        gate_score - jnp.sum(gate_probs * gate_score, axis=-1, keepdims=True)
    )
    logit_low = logit_grad.astype(bf16)
    router_term = dot_tn(normed_two, logit_low)
    normed_two_grad = back_sum[:tok_rows] + dot_nt(logit_low, router_full)
    gain_term_two = jnp.sum(normed_two_grad * residual * scale_two, axis=0)
    weighted = normed_two_grad * gain_two
    residual_grad = (
        cot_float
        + scale_two * weighted
        - residual * scale_two**3 * jnp.mean(weighted * residual, axis=-1, keepdims=True)
    )
    attended_grad = residual_grad.astype(bf16)
    out_term = dot_tn(attended_grad, heads_out)
    context_grad = dot(attended_grad, out_full_t).astype(bf16)
    context_heads = context_grad.reshape(tok_rows, kv_heads, per_group, HEAD_DIM)
    row_delta = jnp.sum(context_heads.astype(f32) * context, axis=-1)

    prob_grad = jnp.einsum("qkgd,nkd->kgqn", context_heads, values, preferred_element_type=f32)
    score_grad = (
        probs.astype(f32) * (prob_grad - jnp.transpose(row_delta, (1, 2, 0))[..., None])
    ).astype(bf16)
    query_rot_grad = (
        jnp.einsum("kgqn,nkd->qkgd", score_grad, keys, preferred_element_type=f32) * score_scale
    )
    key_rot_part = (
        jnp.einsum("kgqn,qkgd->nkd", score_grad, grouped, preferred_element_type=f32)
        * score_scale
    )
    value_part = jnp.einsum("kgqn,qkgd->nkd", probs, context_heads, preferred_element_type=f32)
    key_part = rotary_turn(key_rot_part, cosine, -sine_part)
    kv_pack = jnp.concatenate(
        [key_part.reshape(seq_len, k_cols), value_part.reshape(seq_len, k_cols)], axis=1
    )
    kv_grad = scatter_sum(kv_pack, "context", 0).astype(bf16)
    query_grad = (
        rotary_turn(
            query_rot_grad.reshape(tok_rows, q_heads, HEAD_DIM), local_cos, -local_sin
        )
        .reshape(tok_rows, q_cols)
        .astype(bf16)
    )
    qkv_grad = jnp.concatenate([query_grad, kv_grad], axis=1)
    normed_grad = swap_sum(dot_nt(qkv_grad, qkv_full))
    gain_term_one = jnp.sum(normed_grad * inputs * scale_one, axis=0)
    weighted_one = normed_grad * gain_one
    input_grad = (
        residual_grad
        + scale_one * weighted_one
        - inputs * scale_one**3 * jnp.mean(weighted_one * inputs, axis=-1, keepdims=True)
    )
    qkv_term = dot_tn(normed, qkv_grad).astype(bf16)
    weight_sum_grad = lax.psum_scatter(
        jnp.concatenate([qkv_term, out_term.astype(bf16)], axis=1),
        BOTH,
        scatter_dimension=0,
        tiled=True,
    ).astype(f32)
    small_sum = lax.psum_scatter(
        jnp.concatenate(
            [
                router_term,
                gain_term_one[:, None],
                gain_term_two[:, None],
                jnp.zeros((width, 128 - (experts_total + 2) % 128), f32),
            ],
            axis=1,
        ),
        BOTH,
        scatter_dimension=0,
        tiled=True,
    )
    mixture_sum = swap_sum(mixture)
    output = (residual + mixture_sum).astype(bf16)
    return (
        output,
        input_grad,
        small_sum[:, experts_total],
        weight_sum_grad[:, :q_cols],
        weight_sum_grad[:, q_cols : q_cols + k_cols],
        weight_sum_grad[:, q_cols + k_cols : qkv_cols],
        weight_sum_grad[:, qkv_cols:].T,
        small_sum[:, experts_total + 1],
        small_sum[:, :experts_total],
        grad_expert_gate,
        grad_expert_up,
        grad_expert_down,
    )


def solution(mesh):
    placed = (
        P(("fsdp", "context"), None),
        P(("fsdp", "context"), None),
        P("fsdp", None),
        P(("fsdp", "context"), None),
        P(("fsdp", "context")),
        P(("fsdp", "context"), "tensor"),
        P(("fsdp", "context"), "tensor"),
        P(("fsdp", "context"), "tensor"),
        P("tensor", ("fsdp", "context")),
        P(("fsdp", "context")),
        P(("fsdp", "context"), None),
        P("fsdp", None, "tensor"),
        P("fsdp", None, "tensor"),
        P("fsdp", "tensor", None),
    )
    return jax.shard_map(
        per_device,
        mesh=mesh,
        in_specs=placed,
        out_specs=(
            P(("fsdp", "context"), None),
            P(("fsdp", "context"), None),
            P(("fsdp", "context")),
            P(("fsdp", "context"), "tensor"),
            P(("fsdp", "context"), "tensor"),
            P(("fsdp", "context"), "tensor"),
            P("tensor", ("fsdp", "context")),
            P(("fsdp", "context")),
            P(("fsdp", "context"), None),
            P("fsdp", "context", "tensor"),
            P("fsdp", "context", "tensor"),
            P("fsdp", "tensor", "context"),
        ),
        check_vma=False,
    )
```

time: 2030 us -> 735 us (0.36)
  blocking collectives: 1110 us -> 0 us
  local copies, waits for them, and re-layouts: 194 us -> 44.4 us
  other arithmetic: 159 us -> 48.1 us
  matrix products: 140 us -> 185 us
  waiting for transfers between devices: 394 us -> 421 us
    all_to_all x3 -> x0, blocking collectives: 751 us -> none  [the longest x1 281 us: per_device(): lax.all_to_all(send_grads, 'fsdp', split_axis=0, concat_axis=0, tiled=True)]
    all_gather x7 -> x0, blocking collectives: 286 us -> none  [the longest x1 197 us: per_device(): lax.all_gather(router_weight, ('fsdp', 'context'), axis=0, tiled=True)]
    psum x3 -> x0, waiting for transfers between devices: 125 us -> none  [the longest x1 64 us: per_device(): lax.psum(mixture.astype(jnp.bfloat16), 'tensor').astype(jnp.float32)]
    gather x8 -> x0, local copies, waits for them, and re-layouts: 104 us -> none  [the longest x5 33.6 us: per_device(): selected = jnp.take_along_axis(logits, routes, axis=1)]
    reduce_scatter x8 -> x2, waiting for transfers between devices: 241 us -> 146 us  [the longest x1 79.1 us: per_device(): lax.psum_scatter(mixture_part, 'fsdp', scatter_dimension=0, tiled=True)]
    ppermute x0 -> x9, waiting for transfers between devices: none -> 94.5 us  [the longest x4 53.4 us: swap_sum(): lax.ppermute(low, 'tensor', [(i, (i + step) % count) for i in range(count)])]
    scatter-add x2 -> x0, other arithmetic: 91.6 us -> none  [the longest x1 46.8 us: per_device(): jax.ops.segment_sum(slot_gate[:, None] * flat_out, slot_token, num_segmen...]
    unnamed x17 -> x9, waiting for transfers between devices: 1.63 us -> 81.6 us
  transfers between devices with their start and end apart: 17 -> 16, of which waited for: 11 -> 14; matrix products, arithmetic and copies ran while one was open for 12% -> 20% of each run, Pallas kernels for 0% -> 0%
where the time goes in v1:
time: 735 us; the launch traced here: 729 us
  waiting for transfers between devices  421 us (57%)
  matrix products  185 us (25%)
  other arithmetic  48.1 us (7%)
  local copies, waits for them, and re-layouts  44.4 us (6%)
  between operations  15.4 us (2%)
  starting transfers between devices  15 us (2%)
    unnamed x9, waiting for transfers between devices  81.6 us
    reduce_scatter x1, waiting for transfers between devices, per_device(): lax.psum_scatter(mixture_part, 'fsdp', scatter_dimension=0, tiled=True)  79.1 us
    dot_general x9, matrix products, dot_nt(): lax.dot_general(a, b, (((1,), (1,)), ((), ())), preferred_element_type=f32)  67.8 us
    reduce_scatter x1, waiting for transfers between devices, per_device(): lax.psum_scatter(back_pack.reshape(fsdp_count * (tok_rows + mask_rows), w...  66.7 us
    dot_general x11, matrix products, dot(): return jnp.dot(a, b, preferred_element_type=f32)  59.5 us
    all_gather x1, waiting for transfers between devices, per_device(): all_normed = lax.all_gather(normed_two, 'fsdp', axis=0, tiled=True)  57 us
    ppermute x4, waiting for transfers between devices, swap_sum(): lax.ppermute(low, 'tensor', [(i, (i + step) % count) for i in range(count)])  53.4 us
    dot_general x9, matrix products, dot_tn(): lax.dot_general(a, b, (((0,), (0,)), ((), ())), preferred_element_type=f32)  31.2 us
  transfers between devices with their start and end apart: 16, of which 14 were waited for; matrix products, arithmetic and copies ran while one was open for 20% of the time, Pallas kernels for 0%

profile of v1, /device:TPU:0, one launch (start us, length us, event | category | flops | bytes accessed | tf_op | source)
XLA Modules:
  0.0 729.2 jit_solution(1213884233791044739)
XLA Ops:
  9.6 1.7 concatenate.45
  13.1 2.3 pad_maximum_fusion.3
  15.5 3.0 collective-permute-start
  22.9 22.3 %collective-permute-done = bf16[512,1024]{1,0:T(8,128)(2,1)} collective-permute-done((bf16[512,1024]{1,0:T(8,128)(2,1)S(1)}, bf16[512,1024]{1,0:T(8,128)(2,1)}, u32[]{:S(2)}, u32[]{:S(2)}) %collective-permute-start) | collective-permute-done | bytes 1048608 | tf_op jit(solution)/shard_map/ppermute | solution.py:66
  47.0 15.5 %all-gather.4.cloned.1.call-done = bf16[1024,1664]{1,0:T(8,128)(2,1)} async-done(((bf16[64,1664]{1,0:T(8,128)(2,1)}), bf16[1024,1664]{1,0:T(8,128)(2,1)}) %all-gather.4.cloned.1.call-update) | async-done | bytes 3407888 | tf_op jit(solution)/shard_map/all_gather | solution.py:125
  62.5 1.6 convert_reduce_fusion.1
  68.1 11.8 %fusion.118 = (f32[4,2,512]{2,1,0:T(2,128)S(1)}, f32[4,2,512,1024]{2,3,1,0:T(8,128)}) fusion(pred[512,1024]{0,1:T(8,128)(4,1)} %fusion.22, bf16[512,4,2,32]{0,3,2,1:T(8,128)(2,1)} %bitcast.207, bf16[512,4,2,32]{0,3,2,1:T(8,128)(2,1)S(1)} %bitcast.205, bf16[1024,4,32]{0,2,1:T(8,128)(2,1)S(1)} %get-tuple-element.91, ...), kind=kOutput, calls=%fused_computation.228 | convolution fusion | flops 559940608 | bytes 18366464 | tf_op jit(solution)/shard_map/sub | solution.py:182
  79.9 7.2 divide_convert_fusion
  87.1 3.0 fusion.119
  90.8 2.2 convolution_convert_fusion.2
  92.9 1.6 collective-permute-start.1
  94.5 23.8 %collective-permute-done.1 = bf16[512,1024]{1,0:T(8,128)(2,1)S(1)} collective-permute-done((bf16[512,1024]{1,0:T(8,128)(2,1)S(1)}, bf16[512,1024]{1,0:T(8,128)(2,1)S(1)}, u32[]{:S(2)}, u32[]{:S(2)}) %collective-permute-start.1) | collective-permute-done | bytes 1048608 | tf_op jit(solution)/shard_map/ppermute | solution.py:56
  121.0 26.5 %all-gather.6.cloned.1.call-done = bf16[4160,1024]{1,0:T(8,128)(2,1)} async-done(((bf16[520,1024]{1,0:T(8,128)(2,1)}), bf16[4160,1024]{1,0:T(8,128)(2,1)}) %all-gather.6.cloned.1.call-update) | async-done | bytes 8519696 | tf_op jit(solution)/shard_map/all_gather | solution.py:142
  147.6 7.6 %slice.180 = bf16[8,512,1024]{2,1,0:T(8,128)(2,1)} slice(bf16[8,520,1024]{2,1,0:T(8,128)(2,1)} %bitcast.189), slice={[0:8], [0:512], [0:1024]} | slice | bytes 16777216 | tf_op jit(solution)/shard_map/slice | solution.py:195
  157.5 8.1 %fusion.54 = f32[4096,256]{0,1:T(8,128)} fusion(bf16[4096,1024]{1,0:T(8,128)(2,1)} %bitcast.191, bf16[2,256,1024]{2,1,0:T(8,128)(2,1)} %param.27), kind=kOutput, calls=%fused_computation.130 | convolution fusion | flops 2147483648 | bytes 13107200 | tf_op jit(solution)/shard_map/dot_general | solution.py:44
  165.6 7.8 %fusion.64 = f32[4096,256]{0,1:T(8,128)} fusion(bf16[4096,1024]{1,0:T(8,128)(2,1)} %bitcast.192, bf16[2,256,1024]{2,1,0:T(8,128)(2,1)S(1)} %copy-done.36), kind=kOutput, calls=%fused_computation.140 | convolution fusion | flops 2147483648 | bytes 13107200 | tf_op jit(solution)/shard_map/dot_general | solution.py:44
  173.4 57.0 %all-gather.8.cloned.1.call-done = bf16[4096,1024]{1,0:T(8,128)(2,1)} async-done(((bf16[512,1024]{1,0:T(8,128)(2,1)}), bf16[4096,1024]{1,0:T(8,128)(2,1)}) %all-gather.8.cloned.1.call-update) | async-done | bytes 8388624 | tf_op jit(solution)/shard_map/all_gather | solution.py:193
  230.4 5.8 fusion.120
  236.4 4.6 fusion.58
  241.0 9.0 %multiply_convert_fusion.1 = (bf16[4096,256]{0,1:T(8,128)(2,1)S(1)}, f32[4096]{0:T(1024)S(1)}, bf16[4096,256]{0,1:T(8,128)(2,1)}, bf16[4096,256]{0,1:T(8,128)(2,1)}) fusion(f32[4096,256]{0,1:T(8,128)} %fusion.58, f32[4096,256]{0,1:T(8,128)} %fusion.54, f32[4096]{0:T(1024)S(1)} %bitcast.219, bf16[4096,1024]{1,0:T(8,128)(2,1)S(1)} %copy-done.2, ...), kind=kOutput, calls=%fused_computation.24 | convolution fusion | flops 2167402496 | bytes 23625728 | tf_op jit(solution)/shard_map/dot_general | solution.py:40
  250.0 8.2 %fusion.60 = f32[4096,1024]{1,0:T(8,128)} fusion(bf16[4096,256]{0,1:T(8,128)(2,1)S(1)} %get-tuple-element.78, bf16[2,1024,256]{2,1,0:T(8,128)(2,1)S(1)} %copy-done.38), kind=kOutput, calls=%fused_computation.136 | convolution fusion | flops 2147483648 | bytes 19398656 | tf_op jit(solution)/shard_map/dot_general | solution.py:44
  258.2 4.6 fusion.70
  262.7 8.4 %multiply_convert_fusion.3 = (bf16[4096,256]{0,1:T(8,128)(2,1)S(1)}, f32[4096]{0:T(1024)S(1)}, bf16[4096,256]{0,1:T(8,128)(2,1)S(1)}, bf16[4096,256]{0,1:T(8,128)(2,1)}) fusion(f32[4096,256]{0,1:T(8,128)} %fusion.70, f32[4096,256]{0,1:T(8,128)} %fusion.64, f32[4096]{0:T(1024)S(1)} %bitcast.218, bf16[4096,1024]{1,0:T(8,128)(2,1)S(1)} %copy-done.2, ...), kind=kOutput, calls=%fused_computation.26 | convolution fusion | flops 2167402496 | bytes 23625728 | tf_op jit(solution)/shard_map/dot_general | solution.py:40
  271.1 8.2 %fusion.68 = f32[4096,1024]{1,0:T(8,128)} fusion(bf16[4096,256]{0,1:T(8,128)(2,1)S(1)} %get-tuple-element.82, bf16[2,1024,256]{2,1,0:T(8,128)(2,1)S(1)} %copy-done.35), kind=kOutput, calls=%fused_computation.144 | convolution fusion | flops 2147483648 | bytes 19398656 | tf_op jit(solution)/shard_map/dot_general | solution.py:44
  279.3 8.2 %fusion.72 = f32[4096,1024]{1,0:T(8,128)} fusion(bf16[4096,256]{0,1:T(8,128)(2,1)S(1)} %get-tuple-element.76, bf16[2,1024,256]{2,1,0:T(8,128)(2,1)S(1)} %copy-done.38), kind=kOutput, calls=%fused_computation.148 | convolution fusion | flops 2147483648 | bytes 19398656 | tf_op jit(solution)/shard_map/dot_general | solution.py:44
  287.6 1.9 mul.506
  289.5 3.1 mul.507
  292.7 1.9 mul.497
  294.6 3.8 mul.498
  298.5 21.2 %add_convert_fusion = bf16[4096,1024]{1,0:T(8,128)(2,1)} fusion(f32[4096,1024]{1,0:T(8,128)} %fusion.60, f32[4096,1024]{1,0:T(8,128)} %fusion.72, f32[4096,1024]{1,0:T(8,128)} %fusion.68, bf16[4096,256]{0,1:T(8,128)(2,1)} %get-tuple-element.80, bf16[2,1024,256]{2,1,0:T(8,128)(2,1)S(1)} %copy-done.35), kind=kOutput, calls=%fused_computation.5 | convolution fusion | flops 2164260864 | bytes 61341696 | tf_op jit(solution)/shard_map/dot_general | solution.py:44
  319.8 8.1 %pad_maximum_fusion = bf16[8,520,1024]{2,1,0:T(8,128)(2,1)} fusion(bf16[8,8,1024]{2,1,0:T(8,128)(2,1)S(1)} %add_convert_fusion.6, bf16[8,512,1024]{2,1,0:T(8,128)(2,1)} %bitcast.182), kind=kLoop, calls=%fused_computation.11 | loop fusion | flops 17039360 | bytes 17039360 | tf_op jit(solution)/shard_map/concatenate | solution.py:233
  329.1 9.9 %fusion.66 = f32[4096,1024]{1,0:T(8,128)} fusion(bf16[4096,256]{0,1:T(8,128)(2,1)} %get-tuple-element.83, bf16[2,256,1024]{2,1,0:T(8,128)(2,1)S(1)} %copy-done.37), kind=kOutput, calls=%fused_computation.142 | convolution fusion | flops 2147483648 | bytes 19398656 | tf_op jit(solution)/shard_map/dot_general | solution.py:40
  339.0 11.7 %add_convert_fusion.1 = bf16[4096,1024]{1,0:T(8,128)(2,1)} fusion(f32[4096,1024]{1,0:T(8,128)} %fusion.66, bf16[4096,256]{0,1:T(8,128)(2,1)S(1)} %copy-done.8, bf16[2,256,1024]{2,1,0:T(8,128)(2,1)S(1)} %copy-done.37), kind=kOutput, calls=%fused_computation.6 | convolution fusion | flops 2155872256 | bytes 27787264 | tf_op jit(solution)/shard_map/dot_general | solution.py:40
  350.7 66.7 %reduce-scatter.9.cloned.1.call-done = bf16[520,1024]{1,0:T(8,128)(2,1)} async-done(((bf16[4160,1024]{1,0:T(8,128)(2,1)}), bf16[520,1024]{1,0:T(8,128)(2,1)}) %reduce-scatter.9.cloned.1.call-update) | async-done | bytes 1064976 | tf_op jit(solution)/shard_map/reduce_scatter | solution.py:240
  419.0 1.5 collective-permute-start.3
  420.6 8.1 %convolution_bitcast_fusion = f32[1,256,1024]{2,1,0:T(8,128)} fusion(bf16[4096,256]{0,1:T(8,128)(2,1)} %get-tuple-element.81, bf16[4096,1024]{1,0:T(8,128)(2,1)} %bitcast.193), kind=kOutput, calls=%fused_computation.81 | convolution fusion | flops 2147483648 | bytes 11534336 | tf_op jit(solution)/shard_map/dot_general | solution.py:48
  428.6 79.1 %reduce-scatter.11.cloned.1.call-done = bf16[512,1024]{1,0:T(8,128)(2,1)} async-done(((bf16[4096,1024]{1,0:T(8,128)(2,1)}), bf16[512,1024]{1,0:T(8,128)(2,1)}) %reduce-scatter.11.cloned.1.call-update) | async-done | bytes 1048592 | tf_op jit(solution)/shard_map/reduce_scatter | solution.py:250
  509.2 1.6 convert_add_fusion.1
  512.4 2.6 multiply_reduce_fusion.2
  515.0 15.7 %collective-permute-done.2 = bf16[512,1024]{1,0:T(8,128)(2,1)} collective-permute-done((bf16[512,1024]{1,0:T(8,128)(2,1)}, bf16[512,1024]{1,0:T(8,128)(2,1)}, u32[]{:S(2)}, u32[]{:S(2)}) %collective-permute-start.2) | collective-permute-done | bytes 1048608 | tf_op jit(solution)/shard_map/ppermute | solution.py:56
  530.8 3.9 multiply_subtract_fusion
  534.6 2.2 multiply_reduce_fusion.5
  536.9 2.6 fusion.122
  539.5 4.4 fusion.2
  543.9 3.6 fusion.28
  548.0 1.5 collective-permute-start.4
  549.5 1.5 convolution_multiply_fusion
  551.3 7.3 %collective-permute-done.4 = bf16[512,512]{0,1:T(8,128)(2,1)S(1)} collective-permute-done((bf16[512,512]{0,1:T(8,128)(2,1)S(1)}, bf16[512,512]{0,1:T(8,128)(2,1)S(1)}, u32[]{:S(2)}, u32[]{:S(2)}) %collective-permute-start.4) | collective-permute-done | bytes 524320 | tf_op jit(solution)/shard_map/ppermute | solution.py:83
  562.2 2.4 convolution_bitcast_fusion.1
  567.3 13.9 %collective-permute-done.5 = bf16[512,1024]{1,0:T(8,128)(2,1)S(1)} collective-permute-done((bf16[512,1024]{1,0:T(8,128)(2,1)S(1)}, bf16[512,1024]{1,0:T(8,128)(2,1)S(1)}, u32[]{:S(2)}, u32[]{:S(2)}) %collective-permute-start.5) | collective-permute-done | bytes 1048608 | tf_op jit(solution)/shard_map/ppermute | solution.py:56
  583.0 2.1 copy.98
  585.2 1.9 convolution_convert_fusion.1
  588.4 2.0 pad_maximum_fusion.1
  590.4 4.8 copy.100
  595.3 6.6 convolution_bitcast_fusion.2
  601.9 6.0 convolution_bitcast_fusion.3
  609.5 2.4 convolution_bitcast_fusion.4
  611.9 2.4 convolution_bitcast_fusion.5
  615.0 2.2 fusion.32
  617.2 6.9 collective-permute-done.7
  625.2 4.6 collective-permute-done.6
  630.9 2.1 fusion.16
  632.9 15.9 %reduce-scatter.13.cloned.1.call-done = f32[64,128]{1,0:T(8,128)} async-done(((f32[1024,128]{1,0:T(8,128)}), f32[64,128]{1,0:T(8,128)}) %reduce-scatter.13.cloned.1.call-update) | async-done | bytes 32784
  652.4 65.6 %reduce-scatter.15.cloned.1.call-done = bf16[64,1536]{1,0:T(8,128)(2,1)} async-done(((bf16[1024,1536]{1,0:T(8,128)(2,1)}), bf16[64,1536]{1,0:T(8,128)(2,1)}) %reduce-scatter.15.cloned.1.call-update) | async-done | bytes 196624
  (248 shorter events, 48.3 us)
Async XLA Ops:
  7.2 8.3 %copy-start.3 = (bf16[512,1024]{1,0:T(8,128)(2,1)S(1)}, bf16[512,1024]{1,0:T(8,128)(2,1)}, u32[]{:S(2)}) copy-start(bf16[512,1024]{1,0:T(8,128)(2,1)} %param.14) | copy-start | bytes 3145732
  7.2 11.3 %copy-start.62 = (s32[1,1024]{1,0:T(1,128)S(1)}, s32[1,1024]{1,0:T(1,128)}, u32[]{:S(2)}) copy-start(s32[1,1024]{1,0:T(1,128)} %param.16) | copy-start | bytes 12292
  7.2 55.3 %all-gather.4.cloned.1.call-start = ((), (), s32[]{:S(2)}) async-start(), calls=%async_computation.4 | async-start | bytes 3620864 | tf_op jit(solution)/shard_map/all_gather | solution.py:125
  11.3 136.2 %all-gather.6.cloned.1.call-start = ((), (), s32[]{:S(2)}) async-start(), calls=%async_computation.5 | async-start | bytes 9584640 | tf_op jit(solution)/shard_map/all_gather | solution.py:142
  15.4 214.9 %all-gather.8.cloned.1.call-start = ((), (), s32[]{:S(2)}) async-start(), calls=%async_computation.6 | async-start | bytes 9437184 | tf_op jit(solution)/shard_map/all_gather | solution.py:193
  15.5 29.7 %collective-permute-start = (bf16[512,1024]{1,0:T(8,128)(2,1)S(1)}, bf16[512,1024]{1,0:T(8,128)(2,1)}, u32[]{:S(2)}, u32[]{:S(2)}) collective-permute-start(bf16[512,1024]{1,0:T(8,128)(2,1)S(1)} %copy-done.3), channel_id=1, source_target_pairs={{0,2},{2,0},{1,3},{3,1},{4,6},{6,4},{5,7},{7,5},{8,10},{10,8},{9,1... | collective-permute-start | bytes 3145736 | tf_op jit(solution)/shard_map/ppermute | solution.py:66
  20.3 47.6 %copy-start.32 = (f32[1024,32]{0,1:T(8,128)}, f32[1024,32]{0,1:T(8,128)S(1)}, u32[]{:S(2)}) copy-start(f32[1024,32]{0,1:T(8,128)S(1)} %get-tuple-element.105) | copy-start | bytes 393220
  66.2 20.9 %copy-start.9 = (bf16[1024,256]{0,1:T(8,128)(2,1)}, bf16[1024,256]{0,1:T(8,128)(2,1)S(1)}, u32[]{:S(2)}) copy-start(bf16[1024,256]{0,1:T(8,128)(2,1)S(1)} %slice.287) | copy-start | bytes 1572868
  67.9 12.0 %copy-start.44 = (bf16[512,8,32]{0,2,1:T(8,128)(2,1)}, bf16[512,8,32]{0,2,1:T(8,128)(2,1)S(1)}, u32[]{:S(2)}) copy-start(bf16[512,8,32]{0,2,1:T(8,128)(2,1)S(1)} %get-tuple-element.94) | copy-start | bytes 786436
  68.0 11.8 %copy-start.40 = (bf16[1024,4,32]{0,2,1:T(8,128)(2,1)}, bf16[1024,4,32]{0,2,1:T(8,128)(2,1)S(1)}, u32[]{:S(2)}) copy-start(bf16[1024,4,32]{0,2,1:T(8,128)(2,1)S(1)} %get-tuple-element.90) | copy-start | bytes 786436
  68.1 11.8 %copy-start.42 = (bf16[1024,4,32]{0,2,1:T(8,128)(2,1)}, bf16[1024,4,32]{0,2,1:T(8,128)(2,1)S(1)}, u32[]{:S(2)}) copy-start(bf16[1024,4,32]{0,2,1:T(8,128)(2,1)S(1)} %get-tuple-element.91) | copy-start | bytes 786436
  87.1 3.6 copy-start
  90.8 3.8 copy-start.27
  92.9 25.4 %collective-permute-start.1 = (bf16[512,1024]{1,0:T(8,128)(2,1)S(1)}, bf16[512,1024]{1,0:T(8,128)(2,1)S(1)}, u32[]{:S(2)}, u32[]{:S(2)}) collective-permute-start(bf16[512,1024]{1,0:T(8,128)(2,1)S(1)} %convolution_convert_fusion.2), channel_id=1, source_target_pairs={{0,1},{1,0},{2,3},{3,2},{4,5},{5,4},{6,7},{7,6},{8,9},{9,8},{10,11... | collective-permute-start | bytes 3145736 | tf_op jit(solution)/shard_map/ppermute | solution.py:56
  119.0 393.4 %copy-start.1 = (f32[512,1024]{1,0:T(8,128)}, f32[512,1024]{1,0:T(8,128)S(1)}, u32[]{:S(2)}) copy-start(f32[512,1024]{1,0:T(8,128)S(1)} %get-tuple-element.75) | copy-start | bytes 6291460
  120.5 297.0 %reduce-scatter.9.cloned.1.call-start = ((), (), s32[]{:S(2)}) async-start(), calls=%async_computation.7 | async-start | bytes 9584640 | tf_op jit(solution)/shard_map/reduce_scatter | solution.py:240
  157.5 8.1 %copy-start.36 = (bf16[2,256,1024]{2,1,0:T(8,128)(2,1)S(1)}, bf16[2,256,1024]{2,1,0:T(8,128)(2,1)}, u32[]{:S(2)}) copy-start(bf16[2,256,1024]{2,1,0:T(8,128)(2,1)} %param.27) | copy-start | bytes 3145732
  173.4 63.0 %copy-start.35 = (bf16[2,1024,256]{2,1,0:T(8,128)(2,1)S(1)}, bf16[2,1024,256]{2,1,0:T(8,128)(2,1)}, u32[]{:S(2)}) copy-start(bf16[2,1024,256]{2,1,0:T(8,128)(2,1)} %param.26) | copy-start | bytes 3145732
  230.4 6.0 copy-start.2
  236.4 4.6 copy-start.38
  250.0 8.2 %copy-start.20 = (bf16[4096,256]{0,1:T(8,128)(2,1)}, bf16[4096,256]{0,1:T(8,128)(2,1)S(1)}, u32[]{:S(2)}) copy-start(bf16[4096,256]{0,1:T(8,128)(2,1)S(1)} %get-tuple-element.78) | copy-start | bytes 6291460
  271.1 8.2 %copy-start.24 = (bf16[4096,256]{0,1:T(8,128)(2,1)}, bf16[4096,256]{0,1:T(8,128)(2,1)S(1)}, u32[]{:S(2)}) copy-start(bf16[4096,256]{0,1:T(8,128)(2,1)S(1)} %get-tuple-element.82) | copy-start | bytes 6291460
  271.1 8.2 %copy-start.22 = (bf16[4096,256]{0,1:T(8,128)(2,1)}, bf16[4096,256]{0,1:T(8,128)(2,1)S(1)}, u32[]{:S(2)}) copy-start(bf16[4096,256]{0,1:T(8,128)(2,1)S(1)} %get-tuple-element.76) | copy-start | bytes 6291460
  298.5 21.3 %copy-start.46 = (f32[8,8,1024]{2,1,0:T(8,128)S(1)}, f32[8,8,1024]{2,1,0:T(8,128)}, u32[]{:S(2)}) copy-start(f32[8,8,1024]{2,1,0:T(8,128)} %mul.498) | copy-start | bytes 786436
  327.9 179.8 %reduce-scatter.11.cloned.1.call-start = ((), (), s32[]{:S(2)}) async-start(), calls=%async_computation.8 | async-start | bytes 9437184 | tf_op jit(solution)/shard_map/reduce_scatter | solution.py:250
  329.1 9.9 %copy-start.8 = (bf16[4096,256]{0,1:T(8,128)(2,1)S(1)}, bf16[4096,256]{0,1:T(8,128)(2,1)}, u32[]{:S(2)}) copy-start(bf16[4096,256]{0,1:T(8,128)(2,1)} %get-tuple-element.81) | copy-start | bytes 6291460
  350.7 66.9 %copy-start.5 = (bf16[512,1024]{1,0:T(8,128)(2,1)S(1)}, bf16[512,1024]{1,0:T(8,128)(2,1)}, u32[]{:S(2)}) copy-start(bf16[512,1024]{1,0:T(8,128)(2,1)} %multiply_convert_fusion.6) | copy-start | bytes 3145732
  350.7 66.9 %copy-start.57 = (pred[512,16]{0,1:T(8,128)(4,1)S(1)}, pred[512,16]{0,1:T(8,128)(4,1)}, u32[]{:S(2)}) copy-start(pred[512,16]{0,1:T(8,128)(4,1)} %copy-done.56) | copy-start | bytes 24580
  417.5 231.4 %reduce-scatter.13.cloned.1.call-start = ((), (), s32[]{:S(2)}) async-start(), calls=%async_computation.9 | async-start | bytes 557056
  419.0 90.2 %collective-permute-start.3 = (bf16[520,1024]{1,0:T(8,128)(2,1)}, bf16[520,1024]{1,0:T(8,128)(2,1)}, u32[]{:S(2)}, u32[]{:S(2)}) collective-permute-start(bf16[520,1024]{1,0:T(8,128)(2,1)} %reduce-scatter.9.cloned.1.call-done), channel_id=1, source_target_pairs={{0,1},{1,0},{2,3},{3,2},{4,5},{5,4},{6,7},{7,6},{8,9},{9,8},{10,11... | collective-permute-start | bytes 3194888 | tf_op jit(solution)/shard_map/ppermute | solution.py:56
  420.6 88.6 %copy-start.34 = (bf16[520,1024]{1,0:T(8,128)(2,1)S(1)}, bf16[520,1024]{1,0:T(8,128)(2,1)}, u32[]{:S(2)}) copy-start(bf16[520,1024]{1,0:T(8,128)(2,1)} %reduce-scatter.9.cloned.1.call-done) | copy-start | bytes 3194884
  507.7 23.1 %collective-permute-start.2 = (bf16[512,1024]{1,0:T(8,128)(2,1)}, bf16[512,1024]{1,0:T(8,128)(2,1)}, u32[]{:S(2)}, u32[]{:S(2)}) collective-permute-start(bf16[512,1024]{1,0:T(8,128)(2,1)} %reduce-scatter.11.cloned.1.call-done), channel_id=1, source_target_pairs={{0,1},{1,0},{2,3},{3,2},{4,5},{5,4},{6,7},{7,6},{8,9},{9,8},{10,11... | collective-permute-start | bytes 3145736 | tf_op jit(solution)/shard_map/ppermute | solution.py:56
  512.3 18.4 %copy-start.10 = (bf16[512,1024]{1,0:T(8,128)(2,1)S(1)}, bf16[512,1024]{1,0:T(8,128)(2,1)}, u32[]{:S(2)}) copy-start(bf16[512,1024]{1,0:T(8,128)(2,1)} %param.15) | copy-start | bytes 3145732
  512.3 18.4 %copy-start.39 = (bf16[512,1024]{1,0:T(8,128)(2,1)S(1)}, bf16[512,1024]{1,0:T(8,128)(2,1)}, u32[]{:S(2)}) copy-start(bf16[512,1024]{1,0:T(8,128)(2,1)} %reduce-scatter.11.cloned.1.call-done) | copy-start | bytes 3145732
  530.7 6.1 slice-start
  530.8 3.9 copy-start.15
  530.8 6.1 slice-start.1
  539.5 4.4 copy-start.45
  543.9 3.6 copy-start.33
  543.9 3.6 copy-start.51
  548.0 3.1 copy-start.50
  548.0 10.7 %collective-permute-start.4 = (bf16[512,512]{0,1:T(8,128)(2,1)S(1)}, bf16[512,512]{0,1:T(8,128)(2,1)S(1)}, u32[]{:S(2)}, u32[]{:S(2)}) collective-permute-start(bf16[512,512]{0,1:T(8,128)(2,1)S(1)} %fusion.42), channel_id=1, source_target_pairs={{0,2},{2,0},{1,3},{3,1},{4,6},{6,4},{5,7},{7,5},{8,10},{10,8},{9,1... | collective-permute-start | bytes 1572872 | tf_op jit(solution)/shard_map/ppermute | solution.py:83
  551.1 7.7 %copy-start.31 = (bf16[1024,1664]{1,0:T(8,128)(2,1)S(1)}, bf16[1024,1664]{1,0:T(8,128)(2,1)}, u32[]{:S(2)}) copy-start(bf16[1024,1664]{1,0:T(8,128)(2,1)} %all-gather.4.cloned.1.call-done) | copy-start | bytes 10223620
  551.1 10.6 %slice-start.4 = ((s8[8388608]{0:T(1024)(128)(4,1)}), s8[4194304]{0:T(1024)(128)(4,1)S(1)}, s32[]{:S(2)}) async-start(s8[8388608]{0:T(1024)(128)(4,1)} %bitcast.194), calls=%async_computation.15 | async-start | bytes 8388608
  551.3 8.8 %copy-start.52 = (bf16[512,8,64]{0,2,1:T(8,128)(2,1)}, bf16[512,8,64]{0,2,1:T(8,128)(2,1)S(1)}, u32[]{:S(2)}) copy-start(bf16[512,8,64]{0,2,1:T(8,128)(2,1)S(1)} %pad_maximum_fusion.9) | copy-start | bytes 1572868
  558.8 3.4 copy-start.26
  560.2 21.0 %copy-start.11 = (bf16[512,1024]{1,0:T(8,128)(2,1)}, bf16[512,1024]{1,0:T(8,128)(2,1)S(1)}, u32[]{:S(2)}) copy-start(bf16[512,1024]{1,0:T(8,128)(2,1)S(1)} %fusion.24) | copy-start | bytes 3145732
  560.2 4.5 copy-start.16
  560.2 6.8 copy-start.6
  560.2 21.0 %collective-permute-start.5 = (bf16[512,1024]{1,0:T(8,128)(2,1)S(1)}, bf16[512,1024]{1,0:T(8,128)(2,1)S(1)}, u32[]{:S(2)}, u32[]{:S(2)}) collective-permute-start(bf16[512,1024]{1,0:T(8,128)(2,1)S(1)} %fusion.24), channel_id=1, source_target_pairs={{0,1},{1,0},{2,3},{3,2},{4,5},{5,4},{6,7},{7,6},{8,9},{9,8},{10,11... | collective-permute-start | bytes 3145736 | tf_op jit(solution)/shard_map/ppermute | solution.py:56
  564.6 17.5 %copy-start.18 = (f32[1,256,1024]{2,1,0:T(8,128)}, f32[1,256,1024]{2,1,0:T(8,128)S(1)}, u32[]{:S(2)}) copy-start(f32[1,256,1024]{2,1,0:T(8,128)S(1)} %convolution_bitcast_fusion.1) | copy-start | bytes 3145732
  564.6 16.5 %copy-start.4 = (bf16[512,1024]{1,0:T(8,128)(2,1)S(1)}, bf16[512,1024]{1,0:T(8,128)(2,1)}, u32[]{:S(2)}) copy-start(bf16[512,1024]{1,0:T(8,128)(2,1)} %param.14) | copy-start | bytes 3145732
  564.7 16.5 %copy-start.61 = (f32[1024]{0:T(1024)S(1)}, f32[1024]{0:T(1024)}, u32[]{:S(2)}) copy-start(f32[1024]{0:T(1024)} %copy-done.60) | copy-start | bytes 12292
  565.5 49.5 %collective-permute-start.8 = (bf16[2,256,512]{2,1,0:T(8,128)(2,1)}, bf16[2,256,512]{2,1,0:T(8,128)(2,1)}, u32[]{:S(2)}, u32[]{:S(2)}) collective-permute-start(bf16[2,256,512]{2,1,0:T(8,128)(2,1)} %fusion.30), channel_id=1, source_target_pairs={{0,2},{2,0},{1,3},{3,1},{4,6},{6,4},{5,7},{7,5},{8,10},{10,8},{9,1... | collective-permute-start | bytes 1572872 | tf_op jit(solution)/shard_map/ppermute | solution.py:83
  585.1 132.8 %reduce-scatter.15.cloned.1.call-start = ((), (), s32[]{:S(2)}) async-start(), calls=%async_computation.10 | async-start | bytes 3342336
  595.2 6.6 copy-start.25
  595.3 14.2 %slice-start.2 = ((s8[8388608]{0:T(1024)(128)(4,1)}), s8[4194304]{0:T(1024)(128)(4,1)S(1)}, s32[]{:S(2)}) async-start(s8[8388608]{0:T(1024)(128)(4,1)} %bitcast.183), calls=%async_computation.13 | async-start | bytes 8388608
  601.8 7.6 %slice-start.3 = ((s8[8388608]{0:T(1024)(128)(4,1)}), s8[4194304]{0:T(1024)(128)(4,1)S(1)}, s32[]{:S(2)}) async-start(s8[8388608]{0:T(1024)(128)(4,1)} %bitcast.183), calls=%async_computation.14 | async-start | bytes 8388608
  601.8 7.6 %copy-start.21 = (bf16[4096,256]{0,1:T(8,128)(2,1)S(1)}, bf16[4096,256]{0,1:T(8,128)(2,1)}, u32[]{:S(2)}) copy-start(bf16[4096,256]{0,1:T(8,128)(2,1)} %copy-done.20) | copy-start | bytes 6291460
  607.9 3.9 copy-start.23
  607.9 16.2 %collective-permute-start.7 = (bf16[2,512,256]{2,1,0:T(8,128)(2,1)S(1)}, bf16[2,512,256]{2,1,0:T(8,128)(2,1)S(1)}, u32[]{:S(2)}, u32[]{:S(2)}) collective-permute-start(bf16[2,512,256]{2,1,0:T(8,128)(2,1)S(1)} %fusion.34), channel_id=1, source_target_pairs={{0,2},{2,0},{1,3},{3,1},{4,6},{6,4},{5,7},{7,5},{8,10},{10,8},{9,1... | collective-permute-start | bytes 1572872 | tf_op jit(solution)/shard_map/ppermute | solution.py:83
  614.4 15.5 %collective-permute-start.6 = (bf16[2,512,256]{2,1,0:T(8,128)(2,1)S(1)}, bf16[2,512,256]{2,1,0:T(8,128)(2,1)S(1)}, u32[]{:S(2)}, u32[]{:S(2)}) collective-permute-start(bf16[2,512,256]{2,1,0:T(8,128)(2,1)S(1)} %fusion.38), channel_id=1, source_target_pairs={{0,2},{2,0},{1,3},{3,1},{4,6},{6,4},{5,7},{7,5},{8,10},{10,8},{9,1... | collective-permute-start | bytes 1572872 | tf_op jit(solution)/shard_map/ppermute | solution.py:83
  617.2 13.7 %copy-start.12 = (bf16[512,1024]{1,0:T(8,128)(2,1)S(1)}, bf16[512,1024]{1,0:T(8,128)(2,1)}, u32[]{:S(2)}) copy-start(bf16[512,1024]{1,0:T(8,128)(2,1)} %copy-done.11) | copy-start | bytes 3145732
  617.2 13.7 %copy-start.14 = (bf16[512,1024]{1,0:T(8,128)(2,1)S(1)}, bf16[512,1024]{1,0:T(8,128)(2,1)}, u32[]{:S(2)}) copy-start(bf16[512,1024]{1,0:T(8,128)(2,1)} %copy-done.13) | copy-start | bytes 3145732
  (21 other events, 37.5 us)
Sparse Core Ops, SparseCore 0:
  11.5 51.0 all-gather.3
  64.2 83.3 all-gather.5
  149.7 80.5 all-gather.7
  328.0 89.3 reduce-scatter.8
  419.7 87.9 reduce-scatter.10
  585.2 63.5 reduce-scatter.12
  652.6 65.2 reduce-scatter.14

commit v2 on v1

--- a/solution.py
+++ b/solution.py
@@ -1,6 +1,10 @@
+import functools
+
 import jax
 import jax.numpy as jnp
 from jax import lax
+from jax.experimental import pallas as pl
+from jax.experimental.pallas import tpu as pltpu
 from jax.sharding import PartitionSpec as P
 
 HEAD_DIM = 64
@@ -59,6 +63,95 @@
     return total
 
 
+def expert_kernel(
+    experts, rows_ref, cot_ref, gate_ref, in_ref, down_ref,
+    grad_ref, mix_ref, score_ref, in_grad_ref, down_grad_ref,
+):
+    rows = rows_ref[...]
+    cot = cot_ref[0]
+    wide = down_ref.shape[0]
+    hid = wide // experts
+
+    @pl.when(pl.program_id(0) == 0)
+    def _():
+        in_grad_ref[...] = jnp.zeros_like(in_grad_ref)
+        down_grad_ref[...] = jnp.zeros_like(down_grad_ref)
+
+    pre = dot(rows, in_ref[...])
+    cot_hid = dot_nt(cot, down_ref[...])
+    gate_pre, up_pre = pre[:, :wide], pre[:, wide:]
+    sig_gate = 1.0 / (1.0 + jnp.exp(-gate_pre))
+    gate_act = gate_pre * sig_gate
+    hidden = gate_act * up_pre
+    gates = jnp.concatenate(
+        [
+            jnp.broadcast_to(gate_ref[:, e : e + 1], (rows.shape[0], hid))
+            for e in range(experts)
+        ],
+        axis=1,
+    )
+    scored = hidden * cot_hid
+    lane = lax.broadcasted_iota(jnp.int32, score_ref.shape, 1)
+    score = jnp.zeros(score_ref.shape, f32)
+    for e in range(experts):
+        total = jnp.sum(scored[:, e * hid : (e + 1) * hid], axis=1, keepdims=True)
+        score = jnp.where(lane == e, total, score)
+    score_ref[...] = score
+    gated = (gates * hidden).astype(bf16)
+    hidden_grad = gates * cot_hid
+    gate_grad = (
+        hidden_grad * up_pre * (sig_gate * (1.0 + gate_pre * (1.0 - sig_gate)))
+    ).astype(bf16)
+    up_grad = (hidden_grad * gate_act).astype(bf16)
+    in_grad = jnp.concatenate([gate_grad, up_grad], axis=1)
+    mix_ref[...] = dot(gated, down_ref[...]).astype(bf16)
+    grad_ref[0] = dot_nt(in_grad, in_ref[...]).astype(bf16)
+    for piece in range(2 * experts):
+        in_grad_ref[piece] += dot_tn(rows, in_grad[:, piece * hid : (piece + 1) * hid])
+    for e in range(experts):
+        down_grad_ref[e] += dot_tn(gated[:, e * hid : (e + 1) * hid], cot)
+
+
+def run_experts(all_normed, cot_got, gates, expert_gate, expert_up, expert_down, block):
+    experts, width, hid = expert_gate.shape
+    tokens = all_normed.shape[0]
+    groups, packed_rows, _ = cot_got.shape
+    wide = experts * hid
+    weights_in = jnp.concatenate(
+        [expert_gate[e] for e in range(experts)] + [expert_up[e] for e in range(experts)], axis=1
+    )
+    weights_down = expert_down.reshape(wide, width)
+    return pl.pallas_call(
+        functools.partial(expert_kernel, experts),
+        grid=(groups,),
+        in_specs=[
+            pl.BlockSpec((block, width), lambda i: (i, 0)),
+            pl.BlockSpec((1, block, width), lambda i: (i, 0, 0)),
+            pl.BlockSpec((block, experts), lambda i: (i, 0)),
+            pl.BlockSpec((width, 2 * wide), lambda i: (0, 0)),
+            pl.BlockSpec((wide, width), lambda i: (0, 0)),
+        ],
+        out_specs=[
+            pl.BlockSpec((1, block, width), lambda i: (i, 0, 0)),
+            pl.BlockSpec((block, width), lambda i: (i, 0)),
+            pl.BlockSpec((block, 128), lambda i: (i, 0)),
+            pl.BlockSpec((2 * experts, width, hid), lambda i: (0, 0, 0)),
+            pl.BlockSpec((experts, hid, width), lambda i: (0, 0, 0)),
+        ],
+        out_shape=[
+            jax.ShapeDtypeStruct((groups, packed_rows, width), bf16),
+            jax.ShapeDtypeStruct((tokens, width), bf16),
+            jax.ShapeDtypeStruct((tokens, 128), f32),
+            jax.ShapeDtypeStruct((2 * experts, width, hid), f32),
+            jax.ShapeDtypeStruct((experts, hid, width), f32),
+        ],
+        compiler_params=pltpu.CompilerParams(vmem_limit_bytes=52 * 2**20),
+        cost_estimate=pl.CostEstimate(
+            flops=18 * tokens * width * wide, bytes_accessed=10 * tokens * width, transcendentals=0
+        ),
+    )(all_normed, cot_got, gates, weights_in, weights_down)
+
+
 def gather_rows(part, axis):
     count = lax.axis_size(axis)
     if count != 2:
@@ -67,6 +160,16 @@
     first = lax.axis_index(axis) == 0
     return jnp.concatenate(
         [jnp.where(first, part, other), jnp.where(first, other, part)], axis=0
+    )
+
+
+def gather_columns(part, axis):
+    if lax.axis_size(axis) != 2:
+        return lax.all_gather(part, axis, axis=1, tiled=True)
+    other = lax.ppermute(part, axis, [(0, 1), (1, 0)])
+    first = lax.axis_index(axis) == 0
+    return jnp.concatenate(
+        [jnp.where(first, part, other), jnp.where(first, other, part)], axis=1
     )
 
 
@@ -81,6 +184,17 @@
     kept = lax.dynamic_slice_in_dim(part, me * half, half, axis=dim)
     sent = lax.dynamic_slice_in_dim(part, (1 - me) * half, half, axis=dim).astype(bf16)
     return kept + lax.ppermute(sent, axis, [(0, 1), (1, 0)]).astype(f32)
+
+
+def context_share(part):
+    fsdp_count, context_count = lax.axis_size("fsdp"), lax.axis_size("context")
+    rows = part.shape[0] // (fsdp_count * context_count)
+    split = part.reshape(fsdp_count, context_count, rows, part.shape[1])
+    return scatter_sum(split, "context", 1).reshape(fsdp_count * rows, part.shape[1]).astype(bf16)
+
+
+def fsdp_share(part):
+    return lax.psum_scatter(part, "fsdp", scatter_dimension=0, tiled=True).astype(f32)
 
 
 def per_device(
@@ -139,8 +253,15 @@
     cot_pack = jnp.concatenate(
         [cotangent, named.astype(bf16).reshape(mask_rows, width)], axis=0
     )
-    cot_got = lax.all_gather(cot_pack, "fsdp", axis=0, tiled=True).reshape(
-        fsdp_count, tok_rows + mask_rows, width
+    tensor_count = lax.axis_size("tensor")
+    share_cols = width // tensor_count
+    cot_share = lax.all_gather(
+        lax.dynamic_slice_in_dim(
+            cot_pack, lax.axis_index("tensor") * share_cols, share_cols, axis=1
+        ),
+        "fsdp",
+        axis=0,
+        tiled=True,
     )
 
     offset = lax.axis_index("context") * tok_rows
@@ -192,7 +313,10 @@
 
     all_normed = lax.all_gather(normed_two, "fsdp", axis=0, tiled=True)
     all_tokens = all_normed.shape[0]
-    all_cot = cot_got[:, :tok_rows].reshape(all_tokens, width)
+    cot_share, _ = lax.optimization_barrier((cot_share, normed_two))
+    cot_got = gather_columns(cot_share, "tensor").reshape(
+        fsdp_count, tok_rows + mask_rows, width
+    )
     all_named = cot_got[:, tok_rows:].reshape(all_tokens, experts_total) > 0
 
     def gates(rows, mask):
@@ -206,36 +330,16 @@
     all_gates = lax.dynamic_slice_in_dim(
         gates(all_normed, all_named), lax.axis_index("fsdp") * local_experts, local_experts, axis=1
     )
-    gate_parts, up_parts, hid_parts, score_parts = [], [], [], []
-    for e in range(local_experts):
-        gate_pre = dot(all_normed, expert_gate[e])
-        up_pre = dot(all_normed, expert_up[e])
-        cot_hid = dot_nt(all_cot, expert_down[e])
-        gate_e = all_gates[:, e : e + 1]
-        sig_gate = jax.nn.sigmoid(gate_pre)
-        gate_act = gate_pre * sig_gate
-        hidden = gate_act * up_pre
-        score_parts.append(jnp.sum(hidden * cot_hid, axis=1, keepdims=True))
-        hid_parts.append((gate_e * hidden).astype(bf16))
-        hidden_grad = gate_e * cot_hid
-        gate_parts.append(
-            (hidden_grad * up_pre * sig_gate * (1.0 + gate_pre * (1.0 - sig_gate))).astype(bf16)
-        )
-        up_parts.append((hidden_grad * gate_act).astype(bf16))
+    back_pack, mixture_part, scores_own, in_term, down_term = run_experts(
+        all_normed, cot_got, all_gates, expert_gate, expert_up, expert_down, tok_rows
+    )
     own = lax.axis_index("fsdp") * local_experts + jnp.arange(local_experts, dtype=jnp.int32)
     spread = (own[:, None] == jnp.arange(experts_total, dtype=jnp.int32)[None, :]).astype(f32)
-    score_wide = sum(score_parts[e] * spread[e][None, :] for e in range(local_experts))
-
-    row_grads = sum(
-        dot_nt(gate_parts[e], expert_gate[e]) + dot_nt(up_parts[e], expert_up[e])
-        for e in range(local_experts)
-    ).astype(bf16)
-    back_pack = jnp.concatenate(
-        [
-            row_grads.reshape(fsdp_count, tok_rows, width),
-            score_wide.astype(bf16).reshape(fsdp_count, mask_rows, width),
-        ],
-        axis=1,
+    score_wide = sum(scores_own[:, e : e + 1] * spread[e][None, :] for e in range(local_experts))
+    back_pack = lax.dynamic_update_slice(
+        back_pack,
+        score_wide.astype(bf16).reshape(fsdp_count, mask_rows, width),
+        (0, tok_rows, 0),
     )
     back = lax.psum_scatter(
         back_pack.reshape(fsdp_count * (tok_rows + mask_rows), width),
@@ -243,18 +347,15 @@
         scatter_dimension=0,
         tiled=True,
     )
-    mixture_part = sum(dot(hid_parts[e], expert_down[e]) for e in range(local_experts)).astype(
-        bf16
-    )
-    mixture_part, back = lax.optimization_barrier((mixture_part, back))
+    grad_in = scatter_sum(in_term, "context", 1)
+    grad_expert_gate, grad_expert_up = grad_in[:local_experts], grad_in[local_experts:]
+    grad_expert_down = scatter_sum(down_term, "context", 2)
+    mixture_part, back, grad_expert_gate, grad_expert_up, grad_expert_down = (
+        lax.optimization_barrier(
+            (mixture_part, back, grad_expert_gate, grad_expert_up, grad_expert_down)
+        )
+    )
     mixture = lax.psum_scatter(mixture_part, "fsdp", scatter_dimension=0, tiled=True)
-
-    gate_term = jnp.stack([dot_tn(all_normed, gate_parts[e]) for e in range(local_experts)])
-    up_term = jnp.stack([dot_tn(all_normed, up_parts[e]) for e in range(local_experts)])
-    down_term = jnp.stack([dot_tn(hid_parts[e], all_cot) for e in range(local_experts)])
-    grad_expert_gate = scatter_sum(gate_term, "context", 1)
-    grad_expert_up = scatter_sum(up_term, "context", 1)
-    grad_expert_down = scatter_sum(down_term, "context", 2)
 
     back_sum = swap_sum(back)
     gate_score = back_sum[tok_rows:].reshape(tok_rows, experts_total)
@@ -262,7 +363,7 @@
         gate_score - jnp.sum(gate_probs * gate_score, axis=-1, keepdims=True)
     )
     logit_low = logit_grad.astype(bf16)
-    router_term = dot_tn(normed_two, logit_low)
+    router_term = dot_tn(logit_low, normed_two)
     normed_two_grad = back_sum[:tok_rows] + dot_nt(logit_low, router_full)
     gain_term_two = jnp.sum(normed_two_grad * residual * scale_two, axis=0)
     weighted = normed_two_grad * gain_two
@@ -310,37 +411,30 @@
         + scale_one * weighted_one
         - inputs * scale_one**3 * jnp.mean(weighted_one * inputs, axis=-1, keepdims=True)
     )
-    qkv_term = dot_tn(normed, qkv_grad).astype(bf16)
-    weight_sum_grad = lax.psum_scatter(
-        jnp.concatenate([qkv_term, out_term.astype(bf16)], axis=1),
-        BOTH,
-        scatter_dimension=0,
-        tiled=True,
-    ).astype(f32)
-    small_sum = lax.psum_scatter(
-        jnp.concatenate(
-            [
-                router_term,
-                gain_term_one[:, None],
-                gain_term_two[:, None],
-                jnp.zeros((width, 128 - (experts_total + 2) % 128), f32),
-            ],
-            axis=1,
-        ),
-        BOTH,
-        scatter_dimension=0,
-        tiled=True,
-    )
+    small_rows = jnp.concatenate(
+        [
+            router_term,
+            gain_term_one[None, :],
+            gain_term_two[None, :],
+            jnp.zeros((128 - (experts_total + 2) % 128, width), f32),
+        ],
+        axis=0,
+    )
+    late = context_share(jnp.concatenate([dot_tn(normed, qkv_grad), small_rows.T], axis=1))
+    late, mixture = lax.optimization_barrier((late, mixture))
+    late_sum = fsdp_share(late)
+    qkv_sum, small_sum = late_sum[:, :qkv_cols], late_sum[:, qkv_cols:]
+    out_sum = fsdp_share(context_share(out_term))
     mixture_sum = swap_sum(mixture)
     output = (residual + mixture_sum).astype(bf16)
     return (
         output,
         input_grad,
         small_sum[:, experts_total],
-        weight_sum_grad[:, :q_cols],
-        weight_sum_grad[:, q_cols : q_cols + k_cols],
-        weight_sum_grad[:, q_cols + k_cols : qkv_cols],
-        weight_sum_grad[:, qkv_cols:].T,
+        qkv_sum[:, :q_cols],
+        qkv_sum[:, q_cols : q_cols + k_cols],
+        qkv_sum[:, q_cols + k_cols :],
+        out_sum.T,
         small_sum[:, experts_total + 1],
         small_sum[:, :experts_total],
         grad_expert_gate,

time: 735 us -> 601 us (0.82)
  matrix products: 185 us -> 50.6 us
  waiting for transfers between devices: 421 us -> 321 us
  Pallas kernels: 0 us -> 50.6 us
  other arithmetic: 48.1 us -> 72.5 us
  local copies, waits for them, and re-layouts: 44.4 us -> 66.8 us
    ppermute x0 -> x1, waiting for transfers between devices: none -> 83.3 us  [gather_columns(): other = lax.ppermute(part, axis, [(0, 1), (1, 0)])]
    unnamed x9 -> x7, waiting for transfers between devices: 81.6 us -> 0.11 us
    reduce_scatter x1, waiting for transfers between devices: 79.1 us -> 0.01 us  [per_device(): lax.psum_scatter(mixture_part, 'fsdp', scatter_dimension=0, tiled=True)]
    dot_general x9 -> x3, matrix products: 67.8 us -> 7.08 us  [dot_nt(): lax.dot_general(a, b, (((1,), (1,)), ((), ())), preferred_element_type=f32)]
    all_gather x1, waiting for transfers between devices: 57 us -> 0.01 us  [per_device(): all_normed = lax.all_gather(normed_two, 'fsdp', axis=0, tiled=True)]
    pallas_call x0 -> x1, Pallas kernels: none -> 50.6 us  [run_experts(): pl.pallas_call(functools.partial(expert_kernel, experts), grid=(groups,),...]
    dot_general x11 -> x5, matrix products: 59.5 us -> 12.8 us  [dot(): return jnp.dot(a, b, preferred_element_type=f32)]
    ppermute x4 -> x5, waiting for transfers between devices: 18.8 us -> 58.4 us  [scatter_sum(): return kept + lax.ppermute(sent, axis, [(0, 1), (1, 0)]).astype(f32)]
  transfers between devices with their start and end apart: 16 -> 18, of which waited for: 14 -> 12; matrix products, arithmetic and copies ran while one was open for 20% -> 24% of each run, Pallas kernels for 0% -> 0%
where the time goes in v2:
time: 601 us; the launch traced here: 594 us
  waiting for transfers between devices  321 us (53%)
  other arithmetic  72.5 us (12%)
  local copies, waits for them, and re-layouts  66.8 us (11%)
  matrix products  50.6 us (8%)
  Pallas kernels  50.6 us (8%)
  starting transfers between devices  17.5 us (3%)
  between operations  15 us (2%)
    ppermute x1, waiting for transfers between devices, gather_columns(): other = lax.ppermute(part, axis, [(0, 1), (1, 0)])  83.3 us
    ppermute x5, waiting for transfers between devices, scatter_sum(): return kept + lax.ppermute(sent, axis, [(0, 1), (1, 0)]).astype(f32)  58.4 us
    ppermute x4, waiting for transfers between devices, swap_sum(): lax.ppermute(low, 'tensor', [(i, (i + step) % count) for i in range(count)])  53.2 us
    pallas_call x1, Pallas kernels, run_experts(): pl.pallas_call(functools.partial(expert_kernel, experts), grid=(groups,),...  50.6 us
    reduce_scatter x1, waiting for transfers between devices, per_device(): lax.psum_scatter(back_pack.reshape(fsdp_count * (tok_rows + mask_rows), w...  48.9 us
    reduce_scatter x2, waiting for transfers between devices, fsdp_share(): lax.psum_scatter(part, 'fsdp', scatter_dimension=0, tiled=True).astype(f32)  37.4 us
    mul x11, local copies, waits for them, and re-layouts, per_device(): scores_own[:, e:e + 1] * spread[e][None, :]  21.1 us
    all_gather x1, waiting for transfers between devices, per_device(): full = lax.all_gather(packed, BOTH, axis=0, tiled=True)  20.4 us
  transfers between devices with their start and end apart: 18, of which 12 were waited for; matrix products, arithmetic and copies ran while one was open for 24% of the time, Pallas kernels for 0%

profile of v2, /device:TPU:0, one launch (start us, length us, event | category | flops | bytes accessed | tf_op | source)
XLA Modules:
  0.0 593.8 jit_solution(2523746410983183982)
XLA Ops:
  9.5 1.7 concatenate.48
  11.3 3.0 collective-permute-start
  15.4 1.9 fusion.41
  21.1 19.0 %collective-permute-done = bf16[512,1024]{1,0:T(8,128)(2,1)} collective-permute-done((bf16[512,1024]{1,0:T(8,128)(2,1)}, bf16[512,1024]{1,0:T(8,128)(2,1)}, u32[]{:S(2)}, u32[]{:S(2)}) %collective-permute-start) | collective-permute-done | bytes 1048608 | tf_op jit(solution)/shard_map/ppermute | solution.py:159
  42.0 20.4 %all-gather.4.cloned.1.call-done = bf16[1024,1664]{1,0:T(8,128)(2,1)} async-done(((bf16[64,1664]{1,0:T(8,128)(2,1)}), bf16[1024,1664]{1,0:T(8,128)(2,1)}) %all-gather.4.cloned.1.call-update) | async-done | bytes 3407888 | tf_op jit(solution)/shard_map/all_gather | solution.py:239
  69.9 11.9 %fusion.71 = (f32[4,2,512]{2,1,0:T(2,128)S(1)}, f32[4,2,512,1024]{2,3,1,0:T(8,128)}) fusion(pred[512,1024]{0,1:T(8,128)(4,1)} %fusion.20, bf16[512,4,2,32]{0,3,2,1:T(8,128)(2,1)} %bitcast.145, bf16[512,4,2,32]{0,3,2,1:T(8,128)(2,1)S(1)} %bitcast.143, bf16[1024,4,32]{0,2,1:T(8,128)(2,1)S(1)} %get-tuple-element.113, ...), kind=kOutput, calls=%fused_computation.170 | convolution fusion | flops 559940608 | bytes 18366464 | tf_op jit(solution)/shard_map/sub | solution.py:303
  81.8 7.2 %divide_convert_fusion = bf16[4,2,512,1024]{2,3,1,0:T(8,128)(2,1)S(1)} fusion(f32[4,2,512,1024]{2,3,1,0:T(8,128)} %get-tuple-element.135, f32[4,2,512]{2,1,0:T(2,128)S(1)} %get-tuple-element.134), kind=kLoop, calls=%fused_computation.5 | loop fusion | flops 8388608 | bytes 25182208 | tf_op jit(solution)/shard_map/convert_element_type | solution.py:305
  89.0 3.1 fusion.72
  92.6 2.2 convolution_convert_fusion
  94.7 1.5 collective-permute-start.1
  96.3 23.9 %collective-permute-done.1 = bf16[512,1024]{1,0:T(8,128)(2,1)S(1)} collective-permute-done((bf16[512,1024]{1,0:T(8,128)(2,1)S(1)}, bf16[512,1024]{1,0:T(8,128)(2,1)S(1)}, u32[]{:S(2)}, u32[]{:S(2)}) %collective-permute-start.1) | collective-permute-done | bytes 1048608 | tf_op jit(solution)/shard_map/ppermute | solution.py:60
  124.0 1.5 collective-permute-start.2
  130.8 2.0 slice_bitcast_fusion.1
  132.8 1.7 pad_maximum_fusion.3.in_ref
  134.5 83.3 %collective-permute-done.2 = bf16[4160,512]{1,0:T(8,128)(2,1)} collective-permute-done((bf16[4160,512]{1,0:T(8,128)(2,1)}, bf16[4160,512]{1,0:T(8,128)(2,1)}, u32[]{:S(2)}, u32[]{:S(2)}) %collective-permute-start.2) | collective-permute-done | bytes 4259872 | tf_op jit(solution)/shard_map/ppermute | solution.py:169
  217.8 5.4 broadcast_select_fusion.1
  223.2 8.0 %pad_maximum_fusion = bf16[4160,1024]{1,0:T(8,128)(2,1)} fusion(bf16[4160,512]{1,0:T(8,128)(2,1)} %get-tuple-element.105, bf16[4160,512]{1,0:T(8,128)(2,1)} %get-tuple-element.104), kind=kLoop, calls=%fused_computation.9 | loop fusion | flops 17039360 | bytes 17039360 | tf_op jit(solution)/shard_map/concatenate | solution.py:171
  231.2 1.6 slice_compare_fusion
  232.8 2.4 gt.11
  235.2 6.0 %fusion.73 = (f32[4096]{0:T(1024)S(1)}, f32[4096,16]{1,0:T(8,128)S(1)}) fusion(pred[4096,16]{1,0:T(32,128)(4,1)} %gt.11, bf16[4096,1024]{1,0:T(8,128)(2,1)} %all-gather.6.cloned.1.call-done.rows_ref, bf16[1024,1664]{1,0:T(8,128)(2,1)} %all-gather.4.cloned.1.call-done), kind=kOutput, calls=%fused_computation.172 | convolution fusion | flops 134344704 | bytes 9453568 | tf_op jit(solution)/shard_map/dot_general | solution.py:44
  242.5 2.2 dynamic-slice_divide_fusion.gate_ref
  244.7 50.6 %shard_map.229 = (bf16[8,520,1024]{2,1,0:T(8,128)(2,1)}, bf16[4096,1024]{1,0:T(8,128)(2,1)}, f32[4096,128]{1,0:T(8,128)}, f32[4,1024,256]{2,1,0:T(8,128)}, f32[2,256,1024]{2,1,0:T(8,128)}) custom-call(bf16[4096,1024]{1,0:T(8,128)(2,1)} %all-gather.6.cloned.1.call-done.rows_ref, bf16[8,520,1024]{2,1,0:T(8,128)(2,1)} %bitcast.130, ...), custom_call_target="tpu_custom_call" | custom-call | flops 38654705664 | bytes 41943040 | tf_op jit(solution)/shard_map/pallas_call | solution.py:124
  295.4 4.5 slice_reduce_fusion.1
  301.3 2.7 mul.396
  304.0 3.8 mul.397
  309.3 2.7 mul.404
  311.9 3.8 mul.405
  315.8 1.7 fusion.51
  317.6 1.9 dynamic-slice_convert_fusion.1
  321.1 1.8 collective-permute-start.4
  322.9 31.6 %collective-permute-done.4 = bf16[2,256,512]{2,1,0:T(8,128)(2,1)S(1)} collective-permute-done((bf16[2,256,512]{2,1,0:T(8,128)(2,1)S(1)}, bf16[2,256,512]{2,1,0:T(8,128)(2,1)S(1)}, u32[]{:S(2)}, u32[]{:S(2)}) %collective-permute-start.4) | collective-permute-done | bytes 524320 | tf_op jit(solution)/shard_map/ppermute | solution.py:186
  354.5 2.4 convert_add_fusion.4
  358.6 48.9 %reduce-scatter.5.cloned.1.call-done = bf16[520,1024]{1,0:T(8,128)(2,1)} async-done(((bf16[4160,1024]{1,0:T(8,128)(2,1)}), bf16[520,1024]{1,0:T(8,128)(2,1)}) %reduce-scatter.5.cloned.1.call-update) | async-done | bytes 1064976 | tf_op jit(solution)/shard_map/reduce_scatter | solution.py:344
  407.5 1.5 collective-permute-start.5
  409.6 1.7 fusion.74
  411.9 19.1 %collective-permute-done.5 = bf16[520,1024]{1,0:T(8,128)(2,1)} collective-permute-done((bf16[520,1024]{1,0:T(8,128)(2,1)}, bf16[520,1024]{1,0:T(8,128)(2,1)}, u32[]{:S(2)}, u32[]{:S(2)}) %collective-permute-start.5) | collective-permute-done | bytes 1064992 | tf_op jit(solution)/shard_map/ppermute | solution.py:60
  431.0 1.6 convert_add_fusion.1
  434.6 1.6 reshape.264
  436.2 1.7 copy.81
  439.6 2.6 multiply_reduce_fusion.1
  442.3 1.6 convert_bitcast_fusion
  443.9 3.1 multiply_reduce_fusion.3
  447.0 4.1 fusion.2
  451.1 3.7 fusion.26
  455.1 2.6 fusion.75
  457.9 1.5 collective-permute-start.6
  459.4 1.5 convolution_multiply_fusion
  461.2 7.4 %collective-permute-done.6 = bf16[512,512]{0,1:T(8,128)(2,1)S(1)} collective-permute-done((bf16[512,512]{0,1:T(8,128)(2,1)S(1)}, bf16[512,512]{0,1:T(8,128)(2,1)S(1)}, u32[]{:S(2)}, u32[]{:S(2)}) %collective-permute-start.6) | collective-permute-done | bytes 524320 | tf_op jit(solution)/shard_map/ppermute | solution.py:186
  468.9 2.3 fusion.22
  472.6 2.3 copy.86
  474.9 2.3 fusion.77
  482.4 10.2 %collective-permute-done.7 = bf16[512,1024]{1,0:T(8,128)(2,1)} collective-permute-done((bf16[512,1024]{1,0:T(8,128)(2,1)}, bf16[512,1024]{1,0:T(8,128)(2,1)}, u32[]{:S(2)}, u32[]{:S(2)}) %collective-permute-start.7) | collective-permute-done | bytes 1048608 | tf_op jit(solution)/shard_map/ppermute | solution.py:60
  492.6 2.4 fusion.17
  495.1 2.6 pad_maximum_fusion.1
  497.7 6.1 %copy.85 = f32[1024,1152]{1,0:T(8,128)} copy(f32[1024,1152]{0,1:T(8,128)} %pad_maximum_fusion.1) | data formatting | bytes 9437184 | tf_op jit(solution)/shard_map/concatenate | solution.py:423
  503.8 2.9 dynamic-slice_convert_fusion
  508.1 2.3 add_convert_fusion.2
  510.5 19.4 %collective-permute-done.8 = bf16[8,1,64,1152]{3,2,1,0:T(8,128)(2,1)} collective-permute-done((bf16[8,1,64,1152]{3,2,1,0:T(8,128)(2,1)}, bf16[8,1,64,1152]{3,2,1,0:T(8,128)(2,1)}, u32[]{:S(2)}, u32[]{:S(2)}) %collective-permute-start.8) | collective-permute-done | bytes 1179680 | tf_op jit(solution)/shard_map/ppermute | solution.py:186
  530.0 3.3 add_convert_fusion
  534.8 12.6 %reduce-scatter.11.cloned.1.call-done = bf16[64,512]{1,0:T(8,128)(2,1)} async-done(((bf16[512,512]{1,0:T(8,128)(2,1)}), bf16[64,512]{1,0:T(8,128)(2,1)}) %reduce-scatter.11.cloned.1.call-update) | async-done | bytes 65552 | tf_op jit(solution)/shard_map/reduce_scatter | solution.py:197
  547.4 1.5 convert_bitcast_fusion.1
  548.9 4.3 fusion.16
  553.2 2.8 add_convert_fusion.1
  556.0 24.8 %reduce-scatter.9.cloned.1.call-done = bf16[64,1152]{1,0:T(8,128)(2,1)} async-done(((bf16[512,1152]{1,0:T(8,128)(2,1)}), bf16[64,1152]{1,0:T(8,128)(2,1)}) %reduce-scatter.9.cloned.1.call-update) | async-done | bytes 147472 | tf_op jit(solution)/shard_map/reduce_scatter | solution.py:197
  (187 shorter events, 55.0 us)
Async XLA Ops:
  7.2 10.2 %copy-start.37 = (s32[1,1024]{1,0:T(1,128)S(1)}, s32[1,1024]{1,0:T(1,128)}, u32[]{:S(2)}) copy-start(s32[1,1024]{1,0:T(1,128)} %param.16) | copy-start | bytes 12292
  7.2 55.2 %all-gather.4.cloned.1.call-start = ((), (), s32[]{:S(2)}) async-start(), calls=%async_computation.4 | async-start | bytes 3620864 | tf_op jit(solution)/shard_map/all_gather | solution.py:239
  11.2 28.9 %copy-start.3 = (bf16[512,1024]{1,0:T(8,128)(2,1)S(1)}, bf16[512,1024]{1,0:T(8,128)(2,1)}, u32[]{:S(2)}) copy-start(bf16[512,1024]{1,0:T(8,128)(2,1)} %param.14) | copy-start | bytes 3145732
  11.3 112.7 %all-gather.8.cloned.1.call-start = ((), (), s32[]{:S(2)}) async-start(), calls=%async_computation.6 | async-start | bytes 4792320 | tf_op jit(solution)/shard_map/all_gather | solution.py:258
  11.3 28.8 %collective-permute-start = (bf16[512,1024]{1,0:T(8,128)(2,1)}, bf16[512,1024]{1,0:T(8,128)(2,1)}, u32[]{:S(2)}, u32[]{:S(2)}) collective-permute-start(bf16[512,1024]{1,0:T(8,128)(2,1)} %param.14), channel_id=1, source_target_pairs={{0,2},{2,0},{1,3},{3,1},{4,6},{6,4},{5,7},{7,5},{8,10},{10,8},{9,1... | collective-permute-start | bytes 3145736 | tf_op jit(solution)/shard_map/ppermute | solution.py:159
  17.3 217.9 %all-gather.6.cloned.1.call-start = ((), (), s32[]{:S(2)}) async-start(), calls=%async_computation.5 | async-start | bytes 9437184 | tf_op jit(solution)/shard_map/all_gather | solution.py:314
  19.2 1.9 copy-start.24
  19.9 48.6 %copy-start.26 = (f32[512,32]{0,1:T(8,128)}, f32[512,32]{0,1:T(8,128)S(1)}, u32[]{:S(2)}) copy-start(f32[512,32]{0,1:T(8,128)S(1)} %get-tuple-element.145) | copy-start | bytes 196612
  63.8 2.0 copy-start.17
  65.8 1.4 copy-start.15
  67.1 1.3 copy-start.10
  67.2 21.8 %copy-start.7 = (bf16[1024,256]{0,1:T(8,128)(2,1)}, bf16[1024,256]{0,1:T(8,128)(2,1)S(1)}, u32[]{:S(2)}) copy-start(bf16[1024,256]{0,1:T(8,128)(2,1)S(1)} %slice.238) | copy-start | bytes 1572868
  67.2 2.1 copy-start.25
  68.4 1.3 slice-start.2
  69.3 12.5 %copy-start.23 = (bf16[512,8,32]{0,2,1:T(8,128)(2,1)}, bf16[512,8,32]{0,2,1:T(8,128)(2,1)S(1)}, u32[]{:S(2)}) copy-start(bf16[512,8,32]{0,2,1:T(8,128)(2,1)S(1)} %get-tuple-element.116) | copy-start | bytes 786436
  69.9 11.9 %copy-start.21 = (bf16[1024,4,32]{0,2,1:T(8,128)(2,1)}, bf16[1024,4,32]{0,2,1:T(8,128)(2,1)S(1)}, u32[]{:S(2)}) copy-start(bf16[1024,4,32]{0,2,1:T(8,128)(2,1)S(1)} %get-tuple-element.113) | copy-start | bytes 786436
  89.0 3.6 copy-start.1
  92.6 3.7 copy-start.14
  94.7 25.5 %collective-permute-start.1 = (bf16[512,1024]{1,0:T(8,128)(2,1)S(1)}, bf16[512,1024]{1,0:T(8,128)(2,1)S(1)}, u32[]{:S(2)}, u32[]{:S(2)}) collective-permute-start(bf16[512,1024]{1,0:T(8,128)(2,1)S(1)} %convolution_convert_fusion), channel_id=1, source_target_pairs={{0,1},{1,0},{2,3},{3,2},{4,5},{5,4},{6,7},{7,6},{8,9},{9,8},{10,11... | collective-permute-start | bytes 3145736 | tf_op jit(solution)/shard_map/ppermute | solution.py:60
  123.9 283.6 %reduce-scatter.5.cloned.1.call-start = ((), (), s32[]{:S(2)}) async-start(), calls=%async_computation.7 | async-start | bytes 9584640 | tf_op jit(solution)/shard_map/reduce_scatter | solution.py:344
  124.0 93.8 %collective-permute-start.2 = (bf16[4160,512]{1,0:T(8,128)(2,1)}, bf16[4160,512]{1,0:T(8,128)(2,1)}, u32[]{:S(2)}, u32[]{:S(2)}) collective-permute-start(bf16[4160,512]{1,0:T(8,128)(2,1)} %all-gather.8.cloned.1.call-done), channel_id=1, source_target_pairs={{0,1},{1,0},{2,3},{3,2},{4,5},{5,4},{6,7},{7,6},{8,9},{9,8},{10,11... | collective-permute-start | bytes 12779528 | tf_op jit(solution)/shard_map/ppermute | solution.py:169
  130.8 86.9 %copy-start.9 = (bf16[4160,512]{1,0:T(8,128)(2,1)S(1)}, bf16[4160,512]{1,0:T(8,128)(2,1)}, u32[]{:S(2)}) copy-start(bf16[4160,512]{1,0:T(8,128)(2,1)} %all-gather.8.cloned.1.call-done) | copy-start | bytes 12779524
  235.2 6.0 %copy-start.8 = (pred[4096,16]{1,0:T(32,128)(4,1)S(1)}, pred[4096,16]{1,0:T(32,128)(4,1)}, u32[]{:S(2)}) copy-start(pred[4096,16]{1,0:T(32,128)(4,1)} %gt.11) | copy-start | bytes 196612
  242.5 2.2 copy-start
  317.5 215.8 %reduce-scatter.7.cloned.1.call-start = ((), (), s32[]{:S(2)}) async-start(), calls=%async_computation.8 | async-start | bytes 9437184 | tf_op jit(solution)/shard_map/reduce_scatter | solution.py:358
  317.6 39.3 %copy-start.13 = (f32[4,1024,256]{2,1,0:T(8,128)S(1)}, f32[4,1024,256]{2,1,0:T(8,128)}, u32[]{:S(2)}) copy-start(f32[4,1024,256]{2,1,0:T(8,128)} %get-tuple-element.29) | copy-start | bytes 12582916
  319.5 37.4 %collective-permute-start.3 = (bf16[4,512,256]{2,1,0:T(8,128)(2,1)S(1)}, bf16[4,512,256]{2,1,0:T(8,128)(2,1)S(1)}, u32[]{:S(2)}, u32[]{:S(2)}) collective-permute-start(bf16[4,512,256]{2,1,0:T(8,128)(2,1)S(1)} %dynamic-slice_convert_fusion.1), channel_id=1, source_target_pairs={{0,2},{2,0},{1,3},{3,1},{4,6},{6,4},{5,7},{7,5},{8,10},{10,8},{9,1... | collective-permute-start | bytes 3145736 | tf_op jit(solution)/shard_map/ppermute | solution.py:186
  321.1 33.3 %collective-permute-start.4 = (bf16[2,256,512]{2,1,0:T(8,128)(2,1)S(1)}, bf16[2,256,512]{2,1,0:T(8,128)(2,1)S(1)}, u32[]{:S(2)}, u32[]{:S(2)}) collective-permute-start(bf16[2,256,512]{2,1,0:T(8,128)(2,1)S(1)} %dynamic-slice_convert_fusion.3), channel_id=1, source_target_pairs={{0,2},{2,0},{1,3},{3,1},{4,6},{6,4},{5,7},{7,5},{8,10},{10,8},{9,1... | collective-permute-start | bytes 1572872 | tf_op jit(solution)/shard_map/ppermute | solution.py:186
  407.5 139.9 %reduce-scatter.11.cloned.1.call-start = ((), (), s32[]{:S(2)}) async-start(), calls=%async_computation.10 | async-start | bytes 589824 | tf_op jit(solution)/shard_map/reduce_scatter | solution.py:197
  407.5 23.5 %collective-permute-start.5 = (bf16[520,1024]{1,0:T(8,128)(2,1)}, bf16[520,1024]{1,0:T(8,128)(2,1)}, u32[]{:S(2)}, u32[]{:S(2)}) collective-permute-start(bf16[520,1024]{1,0:T(8,128)(2,1)} %reduce-scatter.5.cloned.1.call-done), channel_id=1, source_target_pairs={{0,1},{1,0},{2,3},{3,2},{4,5},{5,4},{6,7},{7,6},{8,9},{9,8},{10,11... | collective-permute-start | bytes 3194888 | tf_op jit(solution)/shard_map/ppermute | solution.py:60
  409.1 22.0 %copy-start.19 = (bf16[520,1024]{1,0:T(8,128)(2,1)S(1)}, bf16[520,1024]{1,0:T(8,128)(2,1)}, u32[]{:S(2)}) copy-start(bf16[520,1024]{1,0:T(8,128)(2,1)} %reduce-scatter.5.cloned.1.call-done) | copy-start | bytes 3194884
  411.3 0.6 copy-start.33
  411.3 0.6 copy-start.38
  432.6 1.3 copy-start.5
  439.5 2.7 copy-start.35
  439.5 2.7 copy-start.12
  439.5 2.7 copy-start.40
  439.5 2.7 copy-start.42
  439.5 7.4 %slice-start = ((s8[8388608]{0:T(1024)(128)(4,1)}), s8[4194304]{0:T(1024)(128)(4,1)S(1)}, s32[]{:S(2)}) async-start(s8[8388608]{0:T(1024)(128)(4,1)} %bitcast.121), calls=%async_computation.11 | async-start | bytes 8388608
  442.2 1.6 copy-start.11
  442.3 4.7 slice-start.1
  443.9 3.1 copy-start.2
  451.1 3.7 copy-start.28
  457.8 1.7 copy-start.22
  457.9 3.1 copy-start.27
  457.9 3.1 copy-start.34
  457.9 10.8 %collective-permute-start.6 = (bf16[512,512]{0,1:T(8,128)(2,1)S(1)}, bf16[512,512]{0,1:T(8,128)(2,1)S(1)}, u32[]{:S(2)}, u32[]{:S(2)}) collective-permute-start(bf16[512,512]{0,1:T(8,128)(2,1)S(1)} %fusion.28), channel_id=1, source_target_pairs={{0,2},{2,0},{1,3},{3,1},{4,6},{6,4},{5,7},{7,5},{8,10},{10,8},{9,1... | collective-permute-start | bytes 1572872 | tf_op jit(solution)/shard_map/ppermute | solution.py:186
  461.2 7.7 %copy-start.18 = (bf16[1024,1664]{1,0:T(8,128)(2,1)S(1)}, bf16[1024,1664]{1,0:T(8,128)(2,1)}, u32[]{:S(2)}) copy-start(bf16[1024,1664]{1,0:T(8,128)(2,1)} %all-gather.4.cloned.1.call-done) | copy-start | bytes 10223620
  461.2 9.9 %copy-start.29 = (bf16[512,8,64]{0,2,1:T(8,128)(2,1)}, bf16[512,8,64]{0,2,1:T(8,128)(2,1)S(1)}, u32[]{:S(2)}) copy-start(bf16[512,8,64]{0,2,1:T(8,128)(2,1)S(1)} %pad_maximum_fusion.9) | copy-start | bytes 1572868
  468.8 2.3 copy-start.31
  468.9 3.7 copy-start.41
  471.1 21.4 %collective-permute-start.7 = (bf16[512,1024]{1,0:T(8,128)(2,1)}, bf16[512,1024]{1,0:T(8,128)(2,1)}, u32[]{:S(2)}, u32[]{:S(2)}) collective-permute-start(bf16[512,1024]{1,0:T(8,128)(2,1)} %fusion.22), channel_id=1, source_target_pairs={{0,1},{1,0},{2,3},{3,2},{4,5},{5,4},{6,7},{7,6},{8,9},{9,8},{10,11... | collective-permute-start | bytes 3145736 | tf_op jit(solution)/shard_map/ppermute | solution.py:60
  474.9 6.0 %copy-start.4 = (bf16[512,1024]{1,0:T(8,128)(2,1)S(1)}, bf16[512,1024]{1,0:T(8,128)(2,1)}, u32[]{:S(2)}) copy-start(bf16[512,1024]{1,0:T(8,128)(2,1)} %multiply_convert_fusion) | copy-start | bytes 3145732
  474.9 6.0 %copy-start.36 = (bf16[512,16]{0,1:T(8,128)(2,1)S(1)}, bf16[512,16]{0,1:T(8,128)(2,1)}, u32[]{:S(2)}) copy-start(bf16[512,16]{0,1:T(8,128)(2,1)} %copy-done.35) | copy-start | bytes 49156
  474.9 6.2 %copy-start.16 = (bf16[1024,1024]{1,0:T(8,128)(2,1)S(1)}, bf16[1024,1024]{1,0:T(8,128)(2,1)}, u32[]{:S(2)}) copy-start(bf16[1024,1024]{1,0:T(8,128)(2,1)} %copy-done.15) | copy-start | bytes 6291460
  474.9 6.2 %copy-start.30 = (bf16[512,8,64]{0,2,1:T(8,128)(2,1)S(1)}, bf16[512,8,64]{0,2,1:T(8,128)(2,1)}, u32[]{:S(2)}) copy-start(bf16[512,8,64]{0,2,1:T(8,128)(2,1)} %copy-done.29) | copy-start | bytes 1572868
  474.9 6.2 %copy-start.32 = (bf16[512,512]{0,1:T(8,128)(2,1)S(1)}, bf16[512,512]{0,1:T(8,128)(2,1)}, u32[]{:S(2)}) copy-start(bf16[512,512]{0,1:T(8,128)(2,1)} %copy-done.31) | copy-start | bytes 1572868
  477.2 1.3 copy-start.6
  479.3 28.8 %collective-permute-start.10 = (bf16[8,1,64,512]{3,2,1,0:T(8,128)(2,1)}, bf16[8,1,64,512]{3,2,1,0:T(8,128)(2,1)}, u32[]{:S(2)}, u32[]{:S(2)}) collective-permute-start(bf16[8,1,64,512]{3,2,1,0:T(8,128)(2,1)} %dynamic-slice_convert_fusion.2), channel_id=1, source_target_pairs={{0,2},{2,0},{1,3},{3,1},{4,6},{6,4},{5,7},{7,5},{8,10},{10,8},{9,1... | collective-permute-start | bytes 1572872 | tf_op jit(solution)/shard_map/ppermute | solution.py:186
  482.4 12.7 %copy-start.43 = (f32[128]{0:T(128)S(1)}, f32[128]{0:T(128)}, u32[]{:S(2)}) copy-start(f32[128]{0:T(128)} %pad.5.clone) | copy-start | bytes 1540
  506.6 23.3 %collective-permute-start.8 = (bf16[8,1,64,1152]{3,2,1,0:T(8,128)(2,1)}, bf16[8,1,64,1152]{3,2,1,0:T(8,128)(2,1)}, u32[]{:S(2)}, u32[]{:S(2)}) collective-permute-start(bf16[8,1,64,1152]{3,2,1,0:T(8,128)(2,1)} %dynamic-slice_convert_fusion), channel_id=1, source_target_pairs={{0,2},{2,0},{1,3},{3,1},{4,6},{6,4},{5,7},{7,5},{8,10},{10,8},{9,1... | collective-permute-start | bytes 3538952 | tf_op jit(solution)/shard_map/ppermute | solution.py:186
  510.5 70.3 %reduce-scatter.9.cloned.1.call-start = ((), (), s32[]{:S(2)}) async-start(), calls=%async_computation.9 | async-start | bytes 1327104 | tf_op jit(solution)/shard_map/reduce_scatter | solution.py:197
  533.3 19.9 %collective-permute-start.9 = (bf16[512,1024]{1,0:T(8,128)(2,1)}, bf16[512,1024]{1,0:T(8,128)(2,1)}, u32[]{:S(2)}, u32[]{:S(2)}) collective-permute-start(bf16[512,1024]{1,0:T(8,128)(2,1)} %reduce-scatter.7.cloned.1.call-done), channel_id=1, source_target_pairs={{0,1},{1,0},{2,3},{3,2},{4,5},{5,4},{6,7},{7,6},{8,9},{9,8},{10,11... | collective-permute-start | bytes 3145736 | tf_op jit(solution)/shard_map/ppermute | solution.py:60
  548.9 4.3 copy-start.20
  (1 other events, 0.6 us)
Sparse Core Ops, SparseCore 0:
  11.4 50.9 all-gather.3
  64.6 46.7 all-gather.7
  124.0 80.9 all-gather.5
  317.7 89.7 reduce-scatter.4
  409.7 87.9 reduce-scatter.6
  510.6 36.7 reduce-scatter.10
  549.7 31.0 reduce-scatter.8
